TPU v7x, 512 devices: a whole 4x8x8 slice. The times are simulated.
512 devices in a mesh: row: 32 (over y, x), col: 16 (over z, core).
Axes of the slice: x: 4, y: 8, z: 8, core: 2. Of those that a mesh axis runs over, the one named last changes fastest.
Arguments:
- source: float32 [64, 32768], P(None, 'row'), may hold values from -8 to 8
- target: float32 [64, 32768], P(None, 'col'), may hold values from -8 to 8
Outputs:
- source_potential: float32 [32768], P('row')
- target_potential: float32 [32768], P('col')
- mapped: float32 [64, 32768], P(None, 'row')
All inputs are finite; a program needn't handle non-finite values.
Results may differ from a plain program's by a relative error of at most 0.0003.
Values sent between devices are 32-bit elements; how exact they have to be, the bound alone decides.
A program may use at most 64 MiB of HBM per device.

v0:
```python
import jax
import jax.numpy as jnp
from jax import lax
from jax.sharding import PartitionSpec as P

ITERS = 2


EPSILON = 0.005


def normalize(points):
    return points / jnp.sqrt(jnp.sum(points * points, axis=0, keepdims=True) + 1e-06)


def cost_tile(left, right):
    left_sq = jnp.sum(left * left, axis=0)
    right_sq = jnp.sum(right * right, axis=0)
    inner = jnp.dot(
        left.T, right, precision=lax.Precision.HIGHEST, preferred_element_type=jnp.float32
    )
    return left_sq[:, None] + right_sq[None, :] - 2.0 * inner


def split_blocks(points):
    width = points.shape[1]
    block_len = min(256, width)
    count = width // block_len
    return points.reshape(points.shape[0], count, block_len).transpose(1, 0, 2)


def local_partial(left, right, potential):

    def one_block(block):
        scores = (potential[None, :] - cost_tile(block, right)) / EPSILON
        top = jnp.max(scores, axis=1)
        return (top, jnp.sum(jnp.exp(scores - top[:, None]), axis=1))

    tops, totals = lax.map(one_block, split_blocks(left))
    return (tops.reshape(left.shape[1]), totals.reshape(left.shape[1]))


def shards(source, target):
    xs = normalize(source)
    ys = normalize(target)
    count_src = xs.shape[1] * lax.axis_size("row")
    count_tgt = ys.shape[1] * lax.axis_size("col")
    target_potential = jnp.zeros((ys.shape[1],), jnp.float32)
    source_potential = jnp.zeros((xs.shape[1],), jnp.float32)
    for step in range(ITERS):
        local_top, local_total = local_partial(xs, ys, target_potential)
        global_top = lax.pmax(local_top, "col")
        global_total = lax.psum(local_total * jnp.exp(local_top - global_top), "col")
        source_potential = -EPSILON * (
            global_top + jnp.log(global_total) - jnp.log(jnp.float32(count_tgt))
        )
        local_top, local_total = local_partial(ys, xs, source_potential)
        global_top = lax.pmax(local_top, "row")
        global_total = lax.psum(local_total * jnp.exp(local_top - global_top), "row")
        target_potential = -EPSILON * (
            global_top + jnp.log(global_total) - jnp.log(jnp.float32(count_src))
        )

    def map_block(block):
        scores = (target_potential[None, :] - cost_tile(block, ys)) / EPSILON
        top = jnp.max(scores, axis=1)
        weight = jnp.exp(scores - top[:, None])
        numer = jnp.dot(
            ys, weight.T, precision=lax.Precision.HIGHEST, preferred_element_type=jnp.float32
        )
        return (top, numer, jnp.sum(weight, axis=1))

    tops, numers, denoms = lax.map(map_block, split_blocks(xs))
    width = xs.shape[1]
    local_top = tops.reshape(width)
    numer_all = numers.transpose(1, 0, 2).reshape(xs.shape[0], width)
    denom_all = denoms.reshape(width)
    global_top = lax.pmax(local_top, "col")
    rescale = jnp.exp(local_top - global_top)
    stacked = jnp.concatenate(
        [numer_all * rescale[None, :], (denom_all * rescale)[None, :]], axis=0
    )
    summed = lax.psum(stacked, "col")
    mapped = summed[:-1] / summed[-1:]
    return (source_potential, target_potential, mapped)


def solution(mesh):
    placed = (P(None, "row"), P(None, "col"))
    return jax.shard_map(
        shards,
        mesh=mesh,
        in_specs=placed,
        out_specs=(P("row"), P("col"), P(None, "row")),
        check_vma=False,
    )
```

profile of v0, /device:TPU:1, one launch (start us, length us, event | category | flops | bytes accessed | tf_op | source)
XLA Modules:
  0.0 612.5 jit_solution(7449899751378194646)
XLA Ops:
  9.7 11.3 %while.72 = (s32[]{:T(128)}, f32[4,256]{1,0:T(4,128)S(1)}, f32[4,256]{1,0:T(4,128)S(1)}, f32[4,64,256]{2,1,0:T(8,128)S(1)}, f32[2048]{0:T(1024)S(1)}, /*index=5*/f32[64,2048]{1,0:T(8,128)S(1)}, s32[]{:T(128)}, s32[]{:T(128)}) while((s32[]{:T(128)}, f32[4,256]{1,0:T(4,128)S(1)}, f32[4,256]{1,0:T(4,128)S(1)}, f32[4,64,256]{2,1,0:T(8,128)S(1)}, ...), condition=%wide.region_7.8_spmd, body=%wide.region_3.7_spmd.sunk | while | flops 406879488 | bytes 4867173 | solution.py:39
  9.7 2.3 fusion.72
  12.5 2.3 fusion.72
  15.4 2.3 fusion.72
  18.2 2.3 fusion.72
  21.0 30.6 %pmax.35 = f32[1024]{0:T(1024)S(1)} all-reduce(f32[1024]{0:T(1024)S(1)} %bitcast.170), channel_id=1, replica_groups=mesh['row'=32,'col'=16] {'col'}, use_global_device_ids=true, to_apply=%region_8.9 | all-reduce | flops 1024 | bytes 8192 | tf_op jit(solution)/shard_map/pmax | solution.py:52
  51.7 25.8 %psum.35 = f32[1024]{0:T(1024)S(1)} all-reduce(f32[1024]{0:T(1024)S(1)} %exponential_multiply_fusion.3), channel_id=1, replica_groups=mesh['row'=32,'col'=16] {'col'}, use_global_device_ids=true, to_apply=%region_9.10 | all-reduce | flops 1024 | bytes 8192 | tf_op jit(solution)/shard_map/psum | solution.py:53
  77.5 14.0 %while.73 = (s32[]{:T(128)}, f32[8,256]{1,0:T(8,128)S(1)}, f32[8,256]{1,0:T(8,128)S(1)}, f32[1024]{0:T(1024)S(1)}, f32[8,64,256]{2,1,0:T(8,128)S(1)}, /*index=5*...) while((s32[]{:T(128)}, f32[8,256]{1,0:T(8,128)S(1)}, f32[8,256]{1,0:T(8,128)S(1)}, ...), condition=%wide.region_15.16_spmd, body=%wide.region_11.15_spmd.sunk | while | flops 203455744 | bytes 2507885 | solution.py:39
  91.6 62.1 %pmax.36 = f32[2048]{0:T(1024)S(1)} all-reduce(f32[2048]{0:T(1024)S(1)} %bitcast.164), channel_id=1, replica_groups=mesh['row'=32,'col'=16] {'row'}, use_global_device_ids=true, to_apply=%region_16.17 | all-reduce | flops 2048 | bytes 16384 | tf_op jit(solution)/shard_map/pmax | solution.py:58
  153.7 56.8 %psum.36 = f32[2048]{0:T(1024)S(1)} all-reduce(f32[2048]{0:T(1024)S(1)} %exponential_multiply_fusion.1), channel_id=1, replica_groups=mesh['row'=32,'col'=16] {'row'}, use_global_device_ids=true, to_apply=%region_17.18 | all-reduce | flops 2048 | bytes 16384 | tf_op jit(solution)/shard_map/psum | solution.py:59
  210.6 11.4 %while.74 = (s32[]{:T(128)}, f32[4,256]{1,0:T(4,128)S(1)}, f32[4,256]{1,0:T(4,128)S(1)}, f32[2048]{0:T(1024)S(1)}, f32[4,64,256]{2,1,0:T(8,128)S(1)}, /*index=5*...) while((s32[]{:T(128)}, f32[4,256]{1,0:T(4,128)S(1)}, f32[4,256]{1,0:T(4,128)S(1)}, ...), condition=%wide.region_22.23_spmd, body=%wide.region_18.22_spmd.sunk | while | flops 406879488 | bytes 4875373 | solution.py:39
  210.6 2.3 fusion.78
  213.4 2.3 fusion.78
  216.3 2.3 fusion.78
  219.1 2.3 fusion.78
  222.0 51.6 %pmax.37 = f32[1024]{0:T(1024)S(1)} all-reduce(f32[1024]{0:T(1024)S(1)} %bitcast.172), channel_id=1, replica_groups=mesh['row'=32,'col'=16] {'col'}, use_global_device_ids=true, to_apply=%region_23.24 | all-reduce | flops 1024 | bytes 8192 | tf_op jit(solution)/shard_map/pmax | solution.py:52
  273.6 23.6 %psum.37 = f32[1024]{0:T(1024)S(1)} all-reduce(f32[1024]{0:T(1024)S(1)} %exponential_multiply_fusion.2), channel_id=1, replica_groups=mesh['row'=32,'col'=16] {'col'}, use_global_device_ids=true, to_apply=%region_24.25 | all-reduce | flops 1024 | bytes 8192 | tf_op jit(solution)/shard_map/psum | solution.py:53
  297.1 14.0 %while.75 = (s32[]{:T(128)}, f32[8,256]{1,0:T(8,128)S(1)}, f32[8,256]{1,0:T(8,128)S(1)}, f32[1024]{0:T(1024)S(1)}, f32[8,64,256]{2,1,0:T(8,128)S(1)}, /*index=5*...) while((s32[]{:T(128)}, f32[8,256]{1,0:T(8,128)S(1)}, f32[8,256]{1,0:T(8,128)S(1)}, ...), condition=%wide.region_29.30_spmd, body=%wide.region_25.29_spmd.sunk | while | flops 203455744 | bytes 2507885 | solution.py:39
  311.2 59.1 %pmax.38 = f32[2048]{0:T(1024)S(1)} all-reduce(f32[2048]{0:T(1024)S(1)} %bitcast.166), channel_id=1, replica_groups=mesh['row'=32,'col'=16] {'row'}, use_global_device_ids=true, to_apply=%region_30.31 | all-reduce | flops 2048 | bytes 16384 | tf_op jit(solution)/shard_map/pmax | solution.py:58
  370.3 57.2 %psum.38 = f32[2048]{0:T(1024)S(1)} all-reduce(f32[2048]{0:T(1024)S(1)} %exponential_multiply_fusion), channel_id=1, replica_groups=mesh['row'=32,'col'=16] {'row'}, use_global_device_ids=true, to_apply=%region_31.32 | all-reduce | flops 2048 | bytes 16384 | tf_op jit(solution)/shard_map/psum | solution.py:59
  427.6 20.2 %while.76 = (s32[]{:T(128)}, f32[4,256]{1,0:T(4,128)S(1)}, f32[4,64,256]{2,1,0:T(8,128)S(1)}, f32[4,256]{1,0:T(4,128)S(1)}, f32[2048]{0:T(1024)S(1)}, /*index=5*...) while((s32[]{:T(128)}, f32[4,256]{1,0:T(4,128)S(1)}, ...), condition=%wide.region_36.37_spmd, body=%wide.region_32.36_spmd.sunk | while | flops 810056960 | bytes 7563385 | solution.py:73
  427.7 2.3 fusion.85
  430.4 2.2 fusion.86
  432.7 2.3 fusion.85
  435.5 2.2 fusion.86
  437.8 2.3 fusion.85
  440.5 2.2 fusion.86
  442.8 2.3 fusion.85
  445.6 2.2 fusion.86
  447.9 50.7 %pmax.39 = f32[1024]{0:T(1024)S(1)} all-reduce(f32[1024]{0:T(1024)S(1)} %bitcast.168), channel_id=1, replica_groups=mesh['row'=32,'col'=16] {'col'}, use_global_device_ids=true, to_apply=%region_37.38 | all-reduce | flops 1024 | bytes 8192 | tf_op jit(solution)/shard_map/pmax | solution.py:78
  499.4 103.8 %all-reduce.2.cloned.1.call-done = f32[65,1024]{1,0:T(8,128)} async-done(((f32[65,1024]{1,0:T(8,128)}), f32[65,1024]{1,0:T(8,128)}) %all-reduce.2.cloned.1.call-update) | async-done | bytes 266256 | tf_op jit(solution)/shard_map/psum | solution.py:83
  603.9 1.7 slice_divide_fusion
  (179 shorter events, 38.2 us)
Async XLA Ops:
  7.2 2.3 copy-start
  7.2 596.0 %all-reduce.2.cloned.1.call-start = ((), (), s32[]{:S(2)}) async-start(), calls=%async_computation | async-start | bytes 589824 | tf_op jit(solution)/shard_map/psum | solution.py:83
  311.1 116.5 %copy-start.2 = (f32[1024]{0:T(1024)}, f32[1024]{0:T(1024)S(1)}, u32[]{:S(2)}) copy-start(f32[1024]{0:T(1024)S(1)} %get-tuple-element.896) | copy-start | bytes 12292
  447.8 157.8 %copy-start.1 = (f32[2048]{0:T(1024)}, f32[2048]{0:T(1024)S(1)}, u32[]{:S(2)}) copy-start(f32[2048]{0:T(1024)S(1)} %get-tuple-element.894) | copy-start | bytes 24580
Sparse Core Ops, SparseCore 0:
  499.5 103.6 all-reduce.1
where the time goes:
time: 613 us; the launch traced here: 612 us
  blocking collectives  418 us (68%)
  waiting for transfers between devices  104 us (17%)
  matrix products  56.9 us (9%)
  other arithmetic  15.7 us (3%)
  between operations  14.4 us (2%)
    pmax x3, blocking collectives, shards(): global_top = lax.pmax(local_top, 'col')  133 us
    pmax x2, blocking collectives, shards(): global_top = lax.pmax(local_top, 'row')  121 us
    psum x2, blocking collectives, shards(): lax.psum(local_total * jnp.exp(local_top - global_top), 'row')  114 us
    psum x1, waiting for transfers between devices, shards(): summed = lax.psum(stacked, 'col')  104 us
    psum x2, blocking collectives, shards(): lax.psum(local_total * jnp.exp(local_top - global_top), 'col')  49.4 us
    dot_general x28, matrix products, cost_tile(): jnp.dot(left.T, right, precision=lax.Precision.HIGHEST, preferred_element...  48.1 us
  transfers between devices with their start and end apart: 1, of which 1 were waited for; matrix products, arithmetic and copies ran while one was open for 0% of the time, Pallas kernels for 0%

commit v1 on v0

v1 whole, which is shorter than its diff:
```python
import functools
import math

import jax
import jax.numpy as jnp
from jax import lax
from jax.experimental import pallas as pl
from jax.experimental.pallas import tpu as pltpu
from jax.sharding import PartitionSpec as P

MESH = pl.DeviceIdType.MESH
ITERS = 2
EPSILON = 0.005
SCALE = 1.0 / (EPSILON * math.log(2.0))
UNSCALE = EPSILON * math.log(2.0)
LANES = 128
NZ, NX, NY = 8, 4, 8


def normalize(points):
    total = jnp.sum(points * points, axis=0, keepdims=True)
    return points / jnp.sqrt(total + 1e-06)


def split3(a):
    a1 = a.astype(jnp.bfloat16)
    r = a - a1.astype(jnp.float32)
    a2 = r.astype(jnp.bfloat16)
    a3 = (r - a2.astype(jnp.float32)).astype(jnp.bfloat16)
    return a1, a2, a3


def tree(op, xs):
    xs = list(xs)
    while len(xs) > 1:
        xs = [op(xs[i], xs[i + 1]) if i + 1 < len(xs) else xs[i] for i in range(0, len(xs), 2)]
    return xs[0]


def lse2(xs):
    top = tree(jnp.maximum, xs)
    return top + jnp.log2(tree(jnp.add, [jnp.exp2(x - top) for x in xs]))


def kernel(
    n_src_total,
    n_tgt_total,
    src,
    tgt,
    f_out,
    g_out,
    m_out,
    xk,
    yk,
    yt,
    score,
    nx,
    ny,
    gpot,
    fcol,
    part_m,
    part_p,
    a_loc,
    a_pair,
    a_sum,
    a_z,
    b_loc,
    b_x,
    b_sum,
    b_y,
    c_mine,
    c_give,
    c_pair,
    c_sum,
    c_z,
    c_res,
    c_all,
    c_half,
    s_ap,
    r_ap,
    s_az,
    r_az,
    s_bx,
    r_bx,
    s_by,
    r_by,
    s_cp,
    r_cp,
    s_cz,
    r_cz,
    s_cg,
    r_cg,
    s_ch,
    r_ch,
):
    d, ns = src.shape
    nt = tgt.shape[1]
    nsb, ntb = ns // LANES, nt // LANES
    row, col = lax.axis_index("row"), lax.axis_index("col")
    y, x = row // NX, row % NX
    z, core = col // 2, col % 2
    partner = (row, z * 2 + (1 - core))

    def z_peer(o):
        return (row, ((z + o) % NZ) * 2 + core)

    def x_peer(o):
        return (y * NX + (x + o) % NX, col)

    def y_peer(o):
        return (((y + o) % NY) * NX + x, col)

    peers = [partner]
    peers += [z_peer(o) for o in range(1, NZ)]
    peers += [x_peer(o) for o in range(1, NX)]
    peers += [y_peer(o) for o in range(1, NY)]
    barrier = pltpu.get_barrier_semaphore()
    for peer in peers:
        pl.semaphore_signal(barrier, inc=1, device_id=peer, device_id_type=MESH)

    def copy(src_ref, dst_ref, send, recv, peer):
        return pltpu.make_async_remote_copy(
            src_ref=src_ref, dst_ref=dst_ref, send_sem=send, recv_sem=recv,
            device_id=peer, device_id_type=MESH,
        )

    xs = normalize(src[...])
    nx_row = jnp.sum(xs * xs, axis=0, keepdims=True) * SCALE
    for b in range(nsb):
        nx[b : b + 1, :] = nx_row[:, b * LANES : (b + 1) * LANES]
    xs = xs * (2.0 * SCALE)
    first = lax.broadcasted_iota(jnp.int32, (LANES, LANES), 1) < d
    for b in range(nsb):
        blk = xs[:, b * LANES : (b + 1) * LANES]
        both = jnp.concatenate([blk, blk], axis=0).T
        x1 = both.astype(jnp.bfloat16).astype(jnp.float32)
        r = both - x1
        x2 = r.astype(jnp.bfloat16).astype(jnp.float32)
        rows = pl.ds(b * LANES, LANES)
        xk[rows, 0:128] = x1.astype(jnp.bfloat16)
        xk[rows, 128:256] = x2.astype(jnp.bfloat16)
        xk[rows, 256:384] = jnp.where(first, x1, r - x2).astype(jnp.bfloat16)
    ys = normalize(tgt[...])
    ny_row = jnp.sum(ys * ys, axis=0, keepdims=True) * SCALE
    for b in range(ntb):
        ny[b : b + 1, :] = ny_row[:, b * LANES : (b + 1) * LANES]
    y1, y2, y3 = split3(ys)
    for i, part in enumerate((y1, y2, y1, y2, y3, y1)):
        yk[i * d : (i + 1) * d, :] = part
    gpot[...] = -ny[...]
    lane = lax.broadcasted_iota(jnp.int32, (LANES, LANES), 1)
    for b in range(ntb):
        blk = ys[:, b * LANES : (b + 1) * LANES]
        both = jnp.concatenate([blk, blk], axis=0).T
        t1 = both.astype(jnp.bfloat16).astype(jnp.float32)
        r = both - t1
        t2 = r.astype(jnp.bfloat16).astype(jnp.float32)
        rows = pl.ds(b * LANES, LANES)
        yt[rows, 0:128] = jnp.where(first, t1, t2).astype(jnp.bfloat16)
        yt[rows, 128:256] = jnp.where(
            first, r - t2, jnp.where(lane == d, 1.0, 0.0)
        ).astype(jnp.bfloat16)

    def row_pass(with_scores):
        def block(b, _):
            base = pl.multiple_of(b * LANES, LANES)
            if with_scores:
                score[pl.ds(base, LANES), :] = jnp.dot(
                    xk[pl.ds(base, LANES), :], yk[...], preferred_element_type=jnp.float32
                )

            def group(q, _):
                rows = pl.ds(pl.multiple_of(base + q * 16, 16), 16)
                ts = [
                    score[rows, k * LANES : (k + 1) * LANES] + gpot[k : k + 1, :]
                    for k in range(ntb)
                ]
                top = tree(jnp.maximum, ts)
                part_m[rows, :] = top
                part_p[rows, :] = tree(jnp.add, [jnp.exp2(t - top) for t in ts])
                return 0

            lax.fori_loop(0, LANES // 16, group, 0, unroll=2)
            mt = part_m[pl.ds(base, LANES), :].T
            pt = part_p[pl.ds(base, LANES), :].T
            top = jnp.max(mt, axis=0, keepdims=True)
            tot = jnp.sum(pt * jnp.exp2(mt - top), axis=0, keepdims=True)
            a_loc[pl.ds(b, 1), :] = top + jnp.log2(tot)
            return 0

        lax.fori_loop(0, nsb, block, 0)

    def exchange_a(step):
        c = copy(a_loc, a_pair.at[step], s_ap.at[step], r_ap.at[step], partner)
        c.start()
        c.wait_recv()
        a_sum[step] = lse2([a_loc[...], a_pair[step]])
        cs = []
        for o in range(1, NZ):
            cz = copy(
                a_sum.at[step], a_z.at[step, z], s_az.at[step, o - 1], r_az.at[step, o - 1], z_peer(o)
            )
            cz.start()
            cs.append(cz)
        a_z[step, z] = a_sum[step]
        for cz in cs:
            cz.wait_recv()
        pot = math.log2(n_tgt_total) - lse2([a_z[step, i] for i in range(NZ)])
        c.wait_send()
        for cz in cs:
            cz.wait_send()
        return pot

    def col_pass():
        def chunk(k, _):
            lanes = pl.ds(pl.multiple_of(k * LANES, LANES), LANES)
            top = jnp.full((8, LANES), -jnp.inf, jnp.float32)
            acc = jnp.zeros((8, LANES), jnp.float32)
            for b in range(ns // LANES):
                ts = []
                for i in range(LANES // 8):
                    rows = slice(b * LANES + i * 8, b * LANES + (i + 1) * 8)
                    ts.append(score[rows, lanes] + fcol[rows, :])
                new = tree(jnp.maximum, ts)
                if b > 0:
                    new = jnp.maximum(new, top)
                add = tree(jnp.add, [jnp.exp2(t - new) for t in ts])
                acc = acc * jnp.exp2(top - new) + add if b > 0 else add
                top = new
            full = jnp.max(top, axis=0, keepdims=True)
            tot = jnp.sum(acc * jnp.exp2(top - full), axis=0, keepdims=True)
            b_loc[pl.ds(k, 1), :] = full + jnp.log2(tot)
            return 0

        lax.fori_loop(0, ntb, chunk, 0)

    def exchange_b(step):
        cs = []
        for o in range(1, NX):
            cx = copy(
                b_loc, b_x.at[step, x], s_bx.at[step, o - 1], r_bx.at[step, o - 1], x_peer(o)
            )
            cx.start()
            cs.append(cx)
        b_x[step, x] = b_loc[...]
        for cx in cs:
            cx.wait_recv()
        b_sum[step] = lse2([b_x[step, i] for i in range(NX)])
        for o in range(1, NY):
            cy = copy(
                b_sum.at[step], b_y.at[step, y], s_by.at[step, o - 1], r_by.at[step, o - 1], y_peer(o)
            )
            cy.start()
            cs.append(cy)
        b_y[step, y] = b_sum[step]
        for cy in cs[NX - 1 :]:
            cy.wait_recv()
        pot = math.log2(n_src_total) - lse2([b_y[step, i] for i in range(NY)])
        for cx in cs:
            cx.wait_send()
        return pot

    for step in range(ITERS):
        row_pass(step == 0)
        if step == 0:
            pl.semaphore_wait(barrier, len(peers))
        fpot = exchange_a(step)
        if step == ITERS - 1:
            f_out[...] = (fpot + nx[...]) * UNSCALE
        for b in range(nsb):
            fcol[b * LANES : (b + 1) * LANES, :] = jnp.broadcast_to(
                fpot[b : b + 1, :], (LANES, LANES)
            ).T
        col_pass()
        gpot[...] = exchange_b(step)
    g_out[...] = (gpot[...] + ny[...]) * UNSCALE

    half = d // 2

    def pair_copy(t, blk):
        return copy(c_give.at[blk], c_pair.at[blk], s_cp.at[t], r_cp.at[t], partner)

    def z_copy(o, blk):
        return copy(c_sum.at[blk], c_z.at[z], s_cz.at[o], r_cz.at[o], z_peer(o))

    def map_block(t, _):
        blk = (z + 1 + t) % NZ
        base = pl.multiple_of(blk * LANES, LANES)
        res = jnp.zeros((LANES, 2 * LANES), jnp.float32)
        w1s, w2s, tops = [], [], []
        for q in range(LANES // 16):
            rows = pl.ds(pl.multiple_of(base + q * 16, 16), 16)
            ts = [
                score[rows, k * LANES : (k + 1) * LANES] + gpot[k : k + 1, :] for k in range(ntb)
            ]
            top = jnp.max(tree(jnp.maximum, ts), axis=1, keepdims=True)
            w = jnp.concatenate([jnp.exp2(v - top) for v in ts], axis=1)
            w1 = w.astype(jnp.bfloat16)
            w1s.append(w1)
            w2s.append((w - w1.astype(jnp.float32)).astype(jnp.bfloat16))
            tops.append(jnp.broadcast_to(top, (16, LANES)))
        w1 = jnp.concatenate(w1s, axis=0)
        w2 = jnp.concatenate(w2s, axis=0)
        res = jnp.dot(w1, yt[...], preferred_element_type=jnp.float32)
        res += jnp.dot(w2, yt[...], preferred_element_type=jnp.float32)
        lo = res[:, :LANES].T
        hi = jnp.where(lane == d + 1, jnp.concatenate(tops, axis=0), res[:, LANES:]).T
        num = lo[:d] + lo[d:] + hi[:d]
        tail = hi[d : d + 8]
        mine = jnp.where(core == 0, num[:half], num[half:])
        give = jnp.where(core == 0, num[half:], num[:half])
        c_mine[blk, 0:half, :] = mine
        c_mine[blk, half : half + 8, :] = tail
        c_give[blk, 0:half, :] = give
        c_give[blk, half : half + 8, :] = tail
        pair_copy(t, blk).start()
        return 0

    def merge(parts):
        tops = [p[half + 1 : half + 2, :] for p in parts]
        top = tree(jnp.maximum, tops)
        tot = tree(jnp.add, [p[: half + 1, :] * jnp.exp2(v - top) for p, v in zip(parts, tops)])
        return tot, top

    def pair_merge(t, blk):
        pair_copy(t, blk).wait_recv()
        tot, top = merge([c_mine[blk], c_pair[blk]])
        c_sum[blk, 0 : half + 1, :] = tot
        c_sum[blk, half + 1 : half + 2, :] = top

    lax.fori_loop(0, NZ, map_block, 0)

    def send_block(t, _):
        blk = (z + 1 + t) % NZ
        pair_merge(t, blk)
        z_copy(t + 1, blk).start()
        return 0

    lax.fori_loop(0, NZ - 1, send_block, 0)
    pair_merge(NZ - 1, z)
    c_z[z] = c_sum[z]
    for o in range(1, NZ):
        z_copy(o, (z + o) % NZ).wait_recv()
    tot, _ = merge([c_z[i] for i in range(NZ)])
    c_res[...] = tot[:half] / tot[half : half + 1]

    def gather_copy(o):
        return copy(c_res, c_all.at[z], s_cg.at[o], r_cg.at[o], z_peer(o))

    for o in range(1, NZ):
        gather_copy(o).start()
    c_all[z] = c_res[...]
    for o in range(1, NZ):
        gather_copy(o).wait_recv()
    last = copy(c_all, c_half, s_ch.at[0], r_ch.at[0], partner)
    last.start()
    for t in range(NZ):
        pair_copy(t, (z + 1 + t) % NZ).wait_send()
    for o in range(1, NZ):
        z_copy(o, (z + o) % NZ).wait_send()
        gather_copy(o).wait_send()
    last.wait_recv()
    for b in range(NZ):
        own, other = c_all[b], c_half[b]
        lanes = slice(b * LANES, (b + 1) * LANES)
        m_out[0:half, lanes] = jnp.where(core == 0, own, other)
        m_out[half:d, lanes] = jnp.where(core == 0, other, own)
    last.wait_send()


def solution(mesh):
    nrow, ncol = mesh.shape["row"], mesh.shape["col"]

    def shards(source, target):
        d, ns = source.shape
        nt = target.shape[1]
        nsb, ntb = ns // LANES, nt // LANES
        half = d // 2
        f32, bf16 = jnp.float32, jnp.bfloat16
        vmem = pltpu.VMEM
        dma = pltpu.SemaphoreType.DMA
        f, g, m = pl.pallas_call(
            functools.partial(kernel, ns * nrow, nt * ncol),
            out_shape=(
                jax.ShapeDtypeStruct((nsb, LANES), f32),
                jax.ShapeDtypeStruct((ntb, LANES), f32),
                jax.ShapeDtypeStruct((d, ns), f32),
            ),
            in_specs=[pl.BlockSpec(memory_space=vmem)] * 2,
            out_specs=(pl.BlockSpec(memory_space=vmem),) * 3,
            scratch_shapes=[
                vmem((ns, 6 * d), bf16),
                vmem((6 * d, nt), bf16),
                vmem((nt, 2 * LANES), bf16),
                vmem((ns, nt), f32),
                vmem((nsb, LANES), f32),
                vmem((ntb, LANES), f32),
                vmem((ntb, LANES), f32),
                vmem((ns, LANES), f32),
                vmem((ns, LANES), f32),
                vmem((ns, LANES), f32),
                vmem((nsb, LANES), f32),
                vmem((ITERS, nsb, LANES), f32),
                vmem((ITERS, nsb, LANES), f32),
                vmem((ITERS, NZ, nsb, LANES), f32),
                vmem((ntb, LANES), f32),
                vmem((ITERS, NX, ntb, LANES), f32),
                vmem((ITERS, ntb, LANES), f32),
                vmem((ITERS, NY, ntb, LANES), f32),
                vmem((NZ, half + 8, LANES), f32),
                vmem((NZ, half + 8, LANES), f32),
                vmem((NZ, half + 8, LANES), f32),
                vmem((NZ, half + 8, LANES), f32),
                vmem((NZ, half + 8, LANES), f32),
                vmem((half, LANES), f32),
                vmem((NZ, half, LANES), f32),
                vmem((NZ, half, LANES), f32),
                dma((ITERS,)),
                dma((ITERS,)),
                dma((ITERS, NZ - 1)),
                dma((ITERS, NZ - 1)),
                dma((ITERS, NX - 1)),
                dma((ITERS, NX - 1)),
                dma((ITERS, NY - 1)),
                dma((ITERS, NY - 1)),
                dma((NZ,)),
                dma((NZ,)),
                dma((NZ,)),
                dma((NZ,)),
                dma((NZ,)),
                dma((NZ,)),
                dma((1,)),
                dma((1,)),
            ],
            compiler_params=pltpu.CompilerParams(
                collective_id=0, has_side_effects=True, vmem_limit_bytes=40 * 2**20
            ),
            name="sinkhorn",
        )(source, target)
        return f.reshape(ns), g.reshape(nt), m

    return jax.shard_map(
        shards,
        mesh=mesh,
        in_specs=(P(None, "row"), P(None, "col")),
        out_specs=(P("row"), P("col"), P(None, "row")),
        check_vma=False,
    )
```

time: 613 us -> 75.5 us (0.12)
  blocking collectives: 418 us -> 0 us
  waiting for transfers between devices: 104 us -> 0 us
  Pallas kernels: 0 us -> 70.8 us
  matrix products: 56.9 us -> 0 us
  other arithmetic: 15.7 us -> 0 us
  between operations: 14.4 us -> 0.65 us
    pmax x5 -> x0, blocking collectives: 254 us -> none  [the longest x3 133 us: shards(): global_top = lax.pmax(local_top, 'col')]
    psum x4 -> x0, blocking collectives: 163 us -> none  [the longest x2 114 us: shards(): lax.psum(local_total * jnp.exp(local_top - global_top), 'row')]
    psum x1 -> x0, waiting for transfers between devices: 104 us -> none  [shards(): summed = lax.psum(stacked, 'col')]
    pallas_call x0 -> x1, Pallas kernels: none -> 70.8 us  [shards(): pl.pallas_call(functools.partial(kernel, ns * nrow, nt * ncol), out_shape...]
    dot_general x32 -> x0, matrix products: 56.9 us -> none  [the longest x28 48.1 us: cost_tile(): jnp.dot(left.T, right, precision=lax.Precision.HIGHEST, preferred_element...]
    reduce_sum x60 -> x0, other arithmetic: 13.2 us -> none  [the longest x24 8.39 us: one_block(): return (top, jnp.sum(jnp.exp(scores - top[:, None]), axis=1))]
  transfers between devices with their start and end apart: 1 -> 0, of which waited for: 1 -> 0; matrix products, arithmetic and copies ran while one was open for 0% -> 0% of each run, Pallas kernels for 0% -> 0%
where the time goes in v1:
time: 75.5 us; the launch traced here: 75.3 us
  Pallas kernels  70.8 us (94%)
  local copies, waits for them, and re-layouts  3.88 us (5%)
    pallas_call x1, Pallas kernels, shards(): pl.pallas_call(functools.partial(kernel, ns * nrow, nt * ncol), out_shape...  70.8 us
    unnamed x7, local copies, waits for them, and re-layouts  3.88 us

profile of v1, /device:TPU:1, one launch (start us, length us, event | category | flops | bytes accessed | tf_op | source)
XLA Modules:
  0.0 75.3 jit_solution(4650033875616301683)
XLA Ops:
  0.6 0.0 copy-start
  0.6 1.0 %copy-done = f32[64,2048]{1,0:T(8,128)S(1)} copy-done((f32[64,2048]{1,0:T(8,128)S(1)}, f32[64,2048]{1,0:T(8,128)}, u32[]{:S(2)}) %copy-start) | copy-done | bytes 524312
  1.7 0.0 copy-start.1
  1.7 0.9 %copy-done.1 = f32[64,1024]{1,0:T(8,128)S(1)} copy-done((f32[64,1024]{1,0:T(8,128)S(1)}, f32[64,1024]{1,0:T(8,128)}, u32[]{:S(2)}) %copy-start.1) | copy-done | bytes 262168
  2.6 70.8 %sinkhorn.1 = (f32[8,128]{1,0:T(8,128)S(1)}, f32[16,128]{1,0:T(8,128)S(1)}, f32[64,1024]{1,0:T(8,128)S(1)}) custom-call(f32[64,1024]{1,0:T(8,128)S(1)} %copy-done.1, f32[64,2048]{1,0:T(8,128)S(1)} %copy-done), custom_call_target="tpu_custom_call" | custom-call | tf_op jit(solution)/shard_map/sinkhorn/pallas_call | solution.py:382
  73.4 0.6 copy.8
  74.0 0.6 copy.9
  74.6 0.7 copy.10
Async XLA Ops:
  0.6 1.0 %copy-start = (f32[64,2048]{1,0:T(8,128)S(1)}, f32[64,2048]{1,0:T(8,128)}, u32[]{:S(2)}) copy-start(f32[64,2048]{1,0:T(8,128)} %tgt.1) | copy-start | bytes 1572868
  1.7 0.9 %copy-start.1 = (f32[64,1024]{1,0:T(8,128)S(1)}, f32[64,1024]{1,0:T(8,128)}, u32[]{:S(2)}) copy-start(f32[64,1024]{1,0:T(8,128)} %src.1) | copy-start | bytes 786436

commit v2 on v0

v2 whole, which is shorter than its diff:
```python
import functools
import math

import jax
import jax.numpy as jnp
from jax import lax
from jax.experimental import pallas as pl
from jax.experimental.pallas import tpu as pltpu
from jax.sharding import PartitionSpec as P

MESH = pl.DeviceIdType.MESH
ITERS = 2
EPSILON = 0.005
SCALE = 1.0 / (EPSILON * math.log(2.0))
UNSCALE = EPSILON * math.log(2.0)
LANES = 128
NZ, NX, NY = 8, 4, 8
NC, NR = 2 * NZ, NX * NY
ROW_CHUNKS, COL_CHUNKS = 2, 4


def normalize(points):
    total = jnp.sum(points * points, axis=0, keepdims=True)
    return points / jnp.sqrt(total + 1e-06)


def split3(a):
    a1 = a.astype(jnp.bfloat16)
    r = a - a1.astype(jnp.float32)
    a2 = r.astype(jnp.bfloat16)
    a3 = (r - a2.astype(jnp.float32)).astype(jnp.bfloat16)
    return a1, a2, a3


def tree(op, xs):
    xs = list(xs)
    while len(xs) > 1:
        xs = [op(xs[i], xs[i + 1]) if i + 1 < len(xs) else xs[i] for i in range(0, len(xs), 2)]
    return xs[0]


def lse2(xs):
    top = tree(jnp.maximum, xs)
    return top + jnp.log2(tree(jnp.add, [jnp.exp2(x - top) for x in xs]))


def hops(o, n):
    return min(o, n - o)


def kernel(
    n_src_total,
    n_tgt_total,
    src_hbm,
    tgt_hbm,
    f_out,
    g_out,
    m_out,
    src,
    tgt,
    xk,
    yk,
    yt,
    score,
    nx,
    ny,
    gpot,
    fcol,
    part_m,
    part_p,
    a_loc,
    a_all,
    b_loc,
    b_all,
    wbuf,
    c_msg,
    c_in,
    c_res,
    c_all,
    load,
    s_a,
    r_a,
    s_b,
    r_b,
    s_c,
    r_c,
    s_g,
    r_g,
):
    d, ns = src.shape
    nt = tgt.shape[1]
    nsb, ntb = ns // LANES, nt // LANES
    row, col = lax.axis_index("row"), lax.axis_index("col")
    y, x = row // NX, row % NX
    z, core = col // 2, col % 2

    load_src = pltpu.make_async_copy(src_hbm, src, load.at[0])
    load_tgt = pltpu.make_async_copy(tgt_hbm, tgt, load.at[1])
    load_src.start()
    load_tgt.start()

    col_peers = [(o, k) for o in range(NZ) for k in range(2) if (o, k) != (0, 0)]
    col_peers.sort(key=lambda p: -hops(p[0], NZ))
    row_peers = [(o, k) for o in range(NY) for k in range(NX) if (o, k) != (0, 0)]
    row_peers.sort(key=lambda p: -hops(p[0], NY) - hops(p[1], NX))

    def col_peer(o, k):
        return (row, ((z + o) % NZ) * 2 + (core + k) % 2)

    def row_peer(o, k):
        return (((y + o) % NY) * NX + (x + k) % NX, col)

    peers = [col_peer(*p) for p in col_peers] + [row_peer(*p) for p in row_peers]
    barrier = pltpu.get_barrier_semaphore()
    for peer in peers:
        pl.semaphore_signal(barrier, inc=1, device_id=peer, device_id_type=MESH)

    def copy(src_ref, dst_ref, send, recv, peer):
        return pltpu.make_async_remote_copy(
            src_ref=src_ref, dst_ref=dst_ref, send_sem=send, recv_sem=recv,
            device_id=peer, device_id_type=MESH,
        )

    load_src.wait()
    xs = normalize(src[...])
    nx_row = jnp.sum(xs * xs, axis=0, keepdims=True) * SCALE
    for b in range(nsb):
        nx[b : b + 1, :] = nx_row[:, b * LANES : (b + 1) * LANES]
    xs = xs * (2.0 * SCALE)
    first = lax.broadcasted_iota(jnp.int32, (LANES, LANES), 1) < d
    lane = lax.broadcasted_iota(jnp.int32, (LANES, LANES), 1)
    for b in range(nsb):
        blk = xs[:, b * LANES : (b + 1) * LANES]
        both = jnp.concatenate([blk, blk], axis=0).T
        x1 = both.astype(jnp.bfloat16).astype(jnp.float32)
        r = both - x1
        x2 = r.astype(jnp.bfloat16).astype(jnp.float32)
        rows = pl.ds(b * LANES, LANES)
        xk[rows, 0:128] = x1.astype(jnp.bfloat16)
        xk[rows, 128:256] = x2.astype(jnp.bfloat16)
        xk[rows, 256:384] = jnp.where(first, x1, r - x2).astype(jnp.bfloat16)
    load_tgt.wait()
    ys = normalize(tgt[...])
    tgt[...] = ys
    ny_row = jnp.sum(ys * ys, axis=0, keepdims=True) * SCALE
    for b in range(ntb):
        ny[b : b + 1, :] = ny_row[:, b * LANES : (b + 1) * LANES]
    y1, y2, y3 = split3(ys)
    for i, part in enumerate((y1, y2, y1, y2, y3, y1)):
        yk[i * d : (i + 1) * d, :] = part
    gpot[...] = -ny[...]

    def build_map_operand():
        for b in range(ntb):
            blk = tgt[:, b * LANES : (b + 1) * LANES]
            both = jnp.concatenate([blk, blk], axis=0).T
            t1 = both.astype(jnp.bfloat16).astype(jnp.float32)
            r = both - t1
            t2 = r.astype(jnp.bfloat16).astype(jnp.float32)
            rows = pl.ds(b * LANES, LANES)
            yt[rows, 0:128] = jnp.where(first, t1, t2).astype(jnp.bfloat16)
            yt[rows, 128:256] = jnp.where(
                first, r - t2, jnp.where(lane == d, 1.0, 0.0)
            ).astype(jnp.bfloat16)

    def row_pass(step):
        blocks = nsb // ROW_CHUNKS
        size = blocks * LANES
        for c in range(ROW_CHUNKS):
            if step == 0:
                rows = slice(c * size, (c + 1) * size)
                score[rows, :] = jnp.dot(
                    xk[rows, :], yk[...], preferred_element_type=jnp.float32
                )

            def group(q, _):
                rows = pl.ds(pl.multiple_of(c * size + q * 16, 16), 16)
                ts = [
                    score[rows, k * LANES : (k + 1) * LANES] + gpot[k : k + 1, :]
                    for k in range(ntb)
                ]
                top = tree(jnp.maximum, ts)
                part_m[rows, :] = top
                part_p[rows, :] = tree(jnp.add, [jnp.exp2(t - top) for t in ts])
                return 0

            lax.fori_loop(0, size // 16, group, 0, unroll=8)
            for b in range(c * blocks, (c + 1) * blocks):
                mt = part_m[b * LANES : (b + 1) * LANES, :].T
                pt = part_p[b * LANES : (b + 1) * LANES, :].T
                top = jnp.max(mt, axis=0, keepdims=True)
                tot = jnp.sum(pt * jnp.exp2(mt - top), axis=0, keepdims=True)
                a_loc[step, b : b + 1, :] = top + jnp.log2(tot)
            if step == 0 and c == 0:
                pl.semaphore_wait(barrier, len(peers))
            part = pl.ds(c * blocks, blocks)
            for o, k in col_peers:
                copy(
                    a_loc.at[step, part], a_all.at[step, col, part],
                    s_a.at[step], r_a.at[step], col_peer(o, k),
                ).start()

    def finish_a(step):
        a_all[step, col] = a_loc[step]
        got = a_all.at[step, 0 : NC - 1]
        whole = copy(got, got, s_a.at[step], r_a.at[step], peers[0])
        whole.wait_recv()
        pot = math.log2(n_tgt_total) - lse2([a_all[step, i] for i in range(NC)])
        for b in range(nsb):
            fcol[b * LANES : (b + 1) * LANES, :] = jnp.broadcast_to(
                pot[b : b + 1, :], (LANES, LANES)
            ).T
        if step == ITERS - 1:
            f_out[...] = (pot + nx[...]) * UNSCALE

    def col_pass(step):
        blocks = ntb // COL_CHUNKS
        for c in range(COL_CHUNKS):

            def chunk(k, _):
                lanes = pl.ds(pl.multiple_of(k * LANES, LANES), LANES)
                top = acc = None
                for b in range(ns // 64):
                    ts = []
                    for i in range(8):
                        rows = slice(b * 64 + i * 8, b * 64 + (i + 1) * 8)
                        ts.append(score[rows, lanes] + fcol[rows, :])
                    new = tree(jnp.maximum, ts)
                    if b > 0:
                        new = jnp.maximum(new, top)
                    add = tree(jnp.add, [jnp.exp2(t - new) for t in ts])
                    acc = acc * jnp.exp2(top - new) + add if b > 0 else add
                    top = new
                full = jnp.max(top, axis=0, keepdims=True)
                tot = jnp.sum(acc * jnp.exp2(top - full), axis=0, keepdims=True)
                b_loc[step, pl.ds(k, 1), :] = full + jnp.log2(tot)
                return 0

            lax.fori_loop(c * blocks, (c + 1) * blocks, chunk, 0, unroll=2)
            part = pl.ds(c * blocks, blocks)
            for o, k in row_peers:
                copy(
                    b_loc.at[step, part], b_all.at[step, row, part],
                    s_b.at[step], r_b.at[step], row_peer(o, k),
                ).start()

    def finish_b(step):
        b_all[step, row] = b_loc[step]
        got = b_all.at[step, 0 : NR - 1]
        copy(got, got, s_b.at[step], r_b.at[step], peers[0]).wait_recv()
        pot = math.log2(n_src_total) - lse2([b_all[step, i] for i in range(NR)])
        gpot[...] = pot
        if step == ITERS - 1:
            g_out[...] = (pot + ny[...]) * UNSCALE

    for step in range(ITERS):
        row_pass(step)
        if step == 0:
            build_map_operand()
        finish_a(step)
        col_pass(step)
        finish_b(step)

    half = d // 2
    tail = half + 8
    tops_of = [None] * NZ

    def weights(t):
        base = pl.multiple_of((z + 1 + t) % NZ * LANES, LANES)
        tops = []
        for q in range(LANES // 16):
            rows = pl.ds(pl.multiple_of(base + q * 16, 16), 16)
            ts = [
                score[rows, k * LANES : (k + 1) * LANES] + gpot[k : k + 1, :] for k in range(ntb)
            ]
            top = jnp.max(tree(jnp.maximum, ts), axis=1, keepdims=True)
            for k, v in enumerate(ts):
                w = jnp.exp2(v - top)
                w1 = w.astype(jnp.bfloat16)
                lanes = slice(k * LANES, (k + 1) * LANES)
                wbuf[t % 2, q * 16 : (q + 1) * 16, lanes] = w1
                wbuf[t % 2, LANES + q * 16 : LANES + (q + 1) * 16, lanes] = (
                    w - w1.astype(jnp.float32)
                ).astype(jnp.bfloat16)
            tops.append(jnp.broadcast_to(top, (16, LANES)))
        tops_of[t] = jnp.concatenate(tops, axis=0)

    def send_block(t):
        blk = (z + 1 + t) % NZ
        both = jnp.dot(wbuf[t % 2], yt[...], preferred_element_type=jnp.float32)
        res = both[:LANES] + both[LANES:]
        lo = res[:, :LANES].T
        hi = jnp.where(lane == d + 1, tops_of[t], res[:, LANES:]).T
        num = lo[:d] + lo[d:] + hi[:d]
        for k in range(2):
            c_msg[t, k, 0:half, :] = num[k * half : (k + 1) * half]
            c_msg[t, k, half:tail, :] = hi[d : d + 8]
        for k in range(2):
            if (t, k) != (NZ - 1, 0):
                copy(
                    c_msg.at[t, (core + k) % 2], c_in.at[col], s_c.at[0], r_c.at[0],
                    col_peer(t + 1, k),
                ).start()

    weights(0)
    for t in range(NZ):
        if t + 1 < NZ:
            weights(t + 1)
        send_block(t)
    c_in[col] = c_msg[NZ - 1, core]
    got = c_in.at[0 : NC - 1]
    c_whole = copy(got, got, s_c.at[0], r_c.at[0], peers[0])
    c_whole.wait_recv()
    tops = [c_in[i, half + 1 : half + 2, :] for i in range(NC)]
    top = tree(jnp.maximum, tops)
    tot = tree(
        jnp.add, [c_in[i, 0 : half + 1, :] * jnp.exp2(tops[i] - top) for i in range(NC)]
    )
    c_res[...] = tot[:half] / tot[half : half + 1]
    for o, k in col_peers:
        copy(c_res, c_all.at[col], s_g.at[0], r_g.at[0], col_peer(o, k)).start()
    c_all[col] = c_res[...]
    got = c_all.at[0 : NC - 1]
    g_whole = copy(got, got, s_g.at[0], r_g.at[0], peers[0])

    for step in range(ITERS):
        a_got, b_got = a_all.at[step, 0 : NC - 1], b_all.at[step, 0 : NR - 1]
        copy(a_got, a_got, s_a.at[step], r_a.at[step], peers[0]).wait_send()
        copy(b_got, b_got, s_b.at[step], r_b.at[step], peers[0]).wait_send()
    c_whole.wait_send()
    g_whole.wait_recv()
    for i in range(NC):
        m_out[i % 2 * half : (i % 2 + 1) * half, i // 2 * LANES : (i // 2 + 1) * LANES] = c_all[i]
    g_whole.wait_send()


def solution(mesh):
    nrow, ncol = mesh.shape["row"], mesh.shape["col"]

    def shards(source, target):
        d, ns = source.shape
        nt = target.shape[1]
        nsb, ntb = ns // LANES, nt // LANES
        half = d // 2
        f32, bf16 = jnp.float32, jnp.bfloat16
        vmem = pltpu.VMEM
        dma = pltpu.SemaphoreType.DMA
        f, g, m = pl.pallas_call(
            functools.partial(kernel, ns * nrow, nt * ncol),
            out_shape=(
                jax.ShapeDtypeStruct((nsb, LANES), f32),
                jax.ShapeDtypeStruct((ntb, LANES), f32),
                jax.ShapeDtypeStruct((d, ns), f32),
            ),
            in_specs=[pl.BlockSpec(memory_space=pl.ANY)] * 2,
            out_specs=(pl.BlockSpec(memory_space=vmem),) * 3,
            scratch_shapes=[
                vmem((d, ns), f32),
                vmem((d, nt), f32),
                vmem((ns, 6 * d), bf16),
                vmem((6 * d, nt), bf16),
                vmem((nt, 2 * LANES), bf16),
                vmem((ns, nt), f32),
                vmem((nsb, LANES), f32),
                vmem((ntb, LANES), f32),
                vmem((ntb, LANES), f32),
                vmem((ns, LANES), f32),
                vmem((ns, LANES), f32),
                vmem((ns, LANES), f32),
                vmem((ITERS, nsb, LANES), f32),
                vmem((ITERS, NC, nsb, LANES), f32),
                vmem((ITERS, ntb, LANES), f32),
                vmem((ITERS, NR, ntb, LANES), f32),
                vmem((2, 2 * LANES, nt), bf16),
                vmem((NZ, 2, half + 8, LANES), f32),
                vmem((NC, half + 8, LANES), f32),
                vmem((half, LANES), f32),
                vmem((NC, half, LANES), f32),
                dma((2,)),
                dma((ITERS,)),
                dma((ITERS,)),
                dma((ITERS,)),
                dma((ITERS,)),
                dma((1,)),
                dma((1,)),
                dma((1,)),
                dma((1,)),
            ],
            compiler_params=pltpu.CompilerParams(
                collective_id=0, has_side_effects=True, vmem_limit_bytes=40 * 2**20
            ),
            name="sinkhorn",
        )(source, target)
        return f.reshape(ns), g.reshape(nt), m

    return jax.shard_map(
        shards,
        mesh=mesh,
        in_specs=(P(None, "row"), P(None, "col")),
        out_specs=(P("row"), P("col"), P(None, "row")),
        check_vma=False,
    )
```

time: 613 us -> 76.6 us (0.12)
  blocking collectives: 418 us -> 0 us
  waiting for transfers between devices: 104 us -> 0 us
  Pallas kernels: 0 us -> 71.9 us
  matrix products: 56.9 us -> 0 us
  other arithmetic: 15.7 us -> 0 us
  between operations: 14.4 us -> 0.65 us
    pmax x5 -> x0, blocking collectives: 254 us -> none  [the longest x3 133 us: shards(): global_top = lax.pmax(local_top, 'col')]
    psum x4 -> x0, blocking collectives: 163 us -> none  [the longest x2 114 us: shards(): lax.psum(local_total * jnp.exp(local_top - global_top), 'row')]
    psum x1 -> x0, waiting for transfers between devices: 104 us -> none  [shards(): summed = lax.psum(stacked, 'col')]
    pallas_call x0 -> x1, Pallas kernels: none -> 71.9 us  [shards(): pl.pallas_call(functools.partial(kernel, ns * nrow, nt * ncol), out_shape...]
    dot_general x32 -> x0, matrix products: 56.9 us -> none  [the longest x28 48.1 us: cost_tile(): jnp.dot(left.T, right, precision=lax.Precision.HIGHEST, preferred_element...]
    reduce_sum x60 -> x0, other arithmetic: 13.2 us -> none  [the longest x24 8.39 us: one_block(): return (top, jnp.sum(jnp.exp(scores - top[:, None]), axis=1))]
  transfers between devices with their start and end apart: 1 -> 0, of which waited for: 1 -> 0; matrix products, arithmetic and copies ran while one was open for 0% -> 0% of each run, Pallas kernels for 0% -> 0%
where the time goes in v2:
time: 76.6 us; the launch traced here: 76.4 us
  Pallas kernels  71.9 us (94%)
  local copies, waits for them, and re-layouts  3.88 us (5%)
    pallas_call x1, Pallas kernels, shards(): pl.pallas_call(functools.partial(kernel, ns * nrow, nt * ncol), out_shape...  71.9 us
    unnamed x7, local copies, waits for them, and re-layouts  3.88 us

profile of v2, /device:TPU:1, one launch (start us, length us, event | category | flops | bytes accessed | tf_op | source)
XLA Modules:
  0.0 76.4 jit_solution(17762028970180729525)
XLA Ops:
  0.6 0.0 copy-start
  0.6 1.0 %copy-done = f32[64,2048]{1,0:T(8,128)S(1)} copy-done((f32[64,2048]{1,0:T(8,128)S(1)}, f32[64,2048]{1,0:T(8,128)}, u32[]{:S(2)}) %copy-start) | copy-done | bytes 524312
  1.7 0.0 copy-start.1
  1.7 0.9 %copy-done.1 = f32[64,1024]{1,0:T(8,128)S(1)} copy-done((f32[64,1024]{1,0:T(8,128)S(1)}, f32[64,1024]{1,0:T(8,128)}, u32[]{:S(2)}) %copy-start.1) | copy-done | bytes 262168
  2.6 71.9 %sinkhorn.1 = (f32[8,128]{1,0:T(8,128)S(1)}, f32[16,128]{1,0:T(8,128)S(1)}, f32[64,1024]{1,0:T(8,128)S(1)}) custom-call(f32[64,1024]{1,0:T(8,128)S(1)} %copy-done.1, f32[64,2048]{1,0:T(8,128)S(1)} %copy-done), custom_call_target="tpu_custom_call" | custom-call | tf_op jit(solution)/shard_map/sinkhorn/pallas_call | solution.py:348
  74.5 0.6 copy.8
  75.1 0.6 copy.9
  75.7 0.7 copy.10
Async XLA Ops:
  0.6 1.0 %copy-start = (f32[64,2048]{1,0:T(8,128)S(1)}, f32[64,2048]{1,0:T(8,128)}, u32[]{:S(2)}) copy-start(f32[64,2048]{1,0:T(8,128)} %tgt_hbm.1) | copy-start | bytes 1572868
  1.7 0.9 %copy-start.1 = (f32[64,1024]{1,0:T(8,128)S(1)}, f32[64,1024]{1,0:T(8,128)}, u32[]{:S(2)}) copy-start(f32[64,1024]{1,0:T(8,128)} %src_hbm.1) | copy-start | bytes 786436

commit v3 on v2

v3 whole, which is shorter than its diff:
```python
import functools
import math

import jax
import jax.numpy as jnp
from jax import lax
from jax.experimental import pallas as pl
from jax.experimental.pallas import tpu as pltpu
from jax.sharding import PartitionSpec as P

MESH = pl.DeviceIdType.MESH
ITERS = 2
EPSILON = 0.005
SCALE = 1.0 / (EPSILON * math.log(2.0))
UNSCALE = EPSILON * math.log(2.0)
LANES = 128
NZ, NX, NY = 8, 4, 8
NC, NR = 2 * NZ, NX * NY
PARTS = 2


def normalize(points):
    total = jnp.sum(points * points, axis=0, keepdims=True)
    return points / jnp.sqrt(total + 1e-06)


def split3(a):
    a1 = a.astype(jnp.bfloat16)
    r = a - a1.astype(jnp.float32)
    a2 = r.astype(jnp.bfloat16)
    a3 = (r - a2.astype(jnp.float32)).astype(jnp.bfloat16)
    return a1, a2, a3


def tree(op, xs):
    xs = list(xs)
    while len(xs) > 1:
        xs = [op(xs[i], xs[i + 1]) if i + 1 < len(xs) else xs[i] for i in range(0, len(xs), 2)]
    return xs[0]


def lse2(xs):
    top = tree(jnp.maximum, xs)
    return top + jnp.log2(tree(jnp.add, [jnp.exp2(x - top) for x in xs]))


def hops(o, n):
    return min(o, n - o)


def kernel(
    n_src_total,
    n_tgt_total,
    src_hbm,
    tgt_hbm,
    f_out,
    g_out,
    m_out,
    src,
    tgt,
    xk,
    yk,
    yt,
    score,
    nx,
    ny,
    gpot,
    fcol,
    part_m,
    part_p,
    col_m,
    col_p,
    a_loc,
    a_all,
    b_loc,
    b_all,
    wbuf,
    c_mine,
    c_give,
    c_pair,
    c_sum,
    c_in,
    c_res,
    c_all,
    load,
    s_a,
    r_a,
    s_b,
    r_b,
    s_p,
    r_p,
    s_c,
    r_c,
    s_g,
    r_g,
):
    d, ns = src.shape
    nt = tgt.shape[1]
    nsb, ntb = ns // LANES, nt // LANES
    row, col = lax.axis_index("row"), lax.axis_index("col")
    y, x = row // NX, row % NX
    z, core = col // 2, col % 2

    load_src = pltpu.make_async_copy(src_hbm, src, load.at[0])
    load_tgt = pltpu.make_async_copy(tgt_hbm, tgt, load.at[1])
    load_src.start()
    load_tgt.start()

    col_peers = [(o, k) for o in range(NZ) for k in range(2) if (o, k) != (0, 0)]
    col_peers.sort(key=lambda p: -hops(p[0], NZ))
    row_peers = [(o, k) for o in range(NY) for k in range(NX) if (o, k) != (0, 0)]
    row_peers.sort(key=lambda p: -hops(p[0], NY) - hops(p[1], NX))

    def col_peer(o, k):
        return (row, ((z + o) % NZ) * 2 + (core + k) % 2)

    def row_peer(o, k):
        return (((y + o) % NY) * NX + (x + k) % NX, col)

    peers = [col_peer(*p) for p in col_peers] + [row_peer(*p) for p in row_peers]
    barrier = pltpu.get_barrier_semaphore()
    for peer in peers:
        pl.semaphore_signal(barrier, inc=1, device_id=peer, device_id_type=MESH)

    def copy(src_ref, dst_ref, send, recv, peer):
        return pltpu.make_async_remote_copy(
            src_ref=src_ref, dst_ref=dst_ref, send_sem=send, recv_sem=recv,
            device_id=peer, device_id_type=MESH,
        )

    load_src.wait()
    xs = normalize(src[...])
    nx_row = jnp.sum(xs * xs, axis=0, keepdims=True) * SCALE
    for b in range(nsb):
        nx[b : b + 1, :] = nx_row[:, b * LANES : (b + 1) * LANES]
    xs = xs * (2.0 * SCALE)
    first = lax.broadcasted_iota(jnp.int32, (LANES, LANES), 1) < d
    lane = lax.broadcasted_iota(jnp.int32, (LANES, LANES), 1)
    for b in range(nsb):
        blk = xs[:, b * LANES : (b + 1) * LANES]
        both = jnp.concatenate([blk, blk], axis=0).T
        x1 = both.astype(jnp.bfloat16).astype(jnp.float32)
        r = both - x1
        x2 = r.astype(jnp.bfloat16).astype(jnp.float32)
        rows = pl.ds(b * LANES, LANES)
        xk[rows, 0:128] = x1.astype(jnp.bfloat16)
        xk[rows, 128:256] = x2.astype(jnp.bfloat16)
        xk[rows, 256:384] = jnp.where(first, x1, r - x2).astype(jnp.bfloat16)
    load_tgt.wait()
    ys = normalize(tgt[...])
    tgt[...] = ys
    ny_row = jnp.sum(ys * ys, axis=0, keepdims=True) * SCALE
    for b in range(ntb):
        ny[b : b + 1, :] = ny_row[:, b * LANES : (b + 1) * LANES]
    y1, y2, y3 = split3(ys)
    for i, part in enumerate((y1, y2, y1, y2, y3, y1)):
        yk[i * d : (i + 1) * d, :] = part
    gpot[...] = -ny[...]

    def build_map_operand():
        for b in range(ntb):
            blk = tgt[:, b * LANES : (b + 1) * LANES]
            both = jnp.concatenate([blk, blk], axis=0).T
            t1 = both.astype(jnp.bfloat16).astype(jnp.float32)
            r = both - t1
            t2 = r.astype(jnp.bfloat16).astype(jnp.float32)
            rows = pl.ds(b * LANES, LANES)
            yt[rows, 0:128] = jnp.where(first, t1, t2).astype(jnp.bfloat16)
            yt[rows, 128:256] = jnp.where(
                first, r - t2, jnp.where(lane == d, 1.0, 0.0)
            ).astype(jnp.bfloat16)

    def score_tiles(c):
        rows = slice(c * 256, (c + 1) * 256)
        for n in range(nt // 256):
            lanes = slice(n * 256, (n + 1) * 256)

            def tile():
                score[rows, lanes] = jnp.dot(
                    xk[rows, :], yk[:, lanes], preferred_element_type=jnp.float32
                )

            yield tile

    def row_group(base, size, lo, hi, carry):
        rows = pl.ds(base, size)
        ts = [score[rows, k * LANES : (k + 1) * LANES] + gpot[k : k + 1, :] for k in range(lo, hi)]
        top = tree(jnp.maximum, ts)
        if carry:
            old = part_m[rows, :]
            top = jnp.maximum(top, old)
        tot = tree(jnp.add, [jnp.exp2(t - top) for t in ts])
        if carry:
            tot += part_p[rows, :] * jnp.exp2(old - top)
        part_m[rows, :] = top
        part_p[rows, :] = tot

    def send_rows(step, c):
        for i in range(nsb // PARTS):
            b = c * (nsb // PARTS) + i
            mt = part_m[b * LANES : (b + 1) * LANES, :].T
            pt = part_p[b * LANES : (b + 1) * LANES, :].T
            top = jnp.max(mt, axis=0, keepdims=True)
            tot = jnp.sum(pt * jnp.exp2(mt - top), axis=0, keepdims=True)
            a_loc[step, c, i : i + 1, :] = top + jnp.log2(tot)
        if step == 0 and c == 0:
            pl.semaphore_wait(barrier, len(peers))
        for o, k in col_peers:
            copy(
                a_loc.at[step, c], a_all.at[step, c, col],
                s_a.at[step], r_a.at[step, c], col_peer(o, k),
            ).start()

    def first_row_pass():
        count = ns // 256
        for c in range(count + 1):
            tiles = score_tiles(c) if c < count else [lambda: None] * (nt // 256)
            for n, tile in enumerate(tiles):
                tile()
                if c > 0:
                    for q in range(2):
                        row_group((c - 1) * 256 + n * 32 + q * 16, 16, 0, ntb, False)
            if c > 0 and c % (count // PARTS) == 0:
                send_rows(0, c // (count // PARTS) - 1)

    def later_row_pass(step):
        wide = ntb // PARTS
        for c in range(PARTS):
            receive_b(step - 1, c)
            size = ns // PARTS
            for h in range(PARTS):

                def group(q, _):
                    base = pl.multiple_of(h * size + q * 32, 32)
                    row_group(base, 32, c * wide, (c + 1) * wide, c > 0)
                    return 0

                lax.fori_loop(0, size // 32, group, 0, unroll=8)
                if c == PARTS - 1:
                    send_rows(step, h)

    def receive_a(step, c):
        a_all[step, c, col] = a_loc[step, c]
        got = a_all.at[step, c, 0 : NC - 1]
        copy(got, got, s_a.at[step], r_a.at[step, c], peers[0]).wait_recv()
        pot = math.log2(n_tgt_total) - lse2([a_all[step, c, i] for i in range(NC)])
        size = nsb // PARTS
        for i in range(size):
            b = c * size + i
            fcol[b * LANES : (b + 1) * LANES, :] = jnp.broadcast_to(
                pot[i : i + 1, :], (LANES, LANES)
            ).T
        if step == ITERS - 1:
            part = slice(c * size, (c + 1) * size)
            f_out[part, :] = (pot + nx[part, :]) * UNSCALE

    def col_pass(step):
        wide = ntb // PARTS
        size = ns // PARTS
        for h in range(PARTS):
            receive_a(step, h)
            for c in range(PARTS):
                tops, accs = [None] * wide, [None] * wide
                if h > 0:
                    for k in range(wide):
                        lanes = slice((c * wide + k) * LANES, (c * wide + k + 1) * LANES)
                        tops[k], accs[k] = col_m[:, lanes], col_p[:, lanes]
                for b in range(size // 64):
                    for k in range(wide):
                        lanes = slice((c * wide + k) * LANES, (c * wide + k + 1) * LANES)
                        ts = []
                        for i in range(8):
                            at = h * size + b * 64 + i * 8
                            ts.append(score[at : at + 8, lanes] + fcol[at : at + 8, :])
                        new = tree(jnp.maximum, ts)
                        if tops[k] is not None:
                            new = jnp.maximum(new, tops[k])
                        add = tree(jnp.add, [jnp.exp2(t - new) for t in ts])
                        if tops[k] is not None:
                            add += accs[k] * jnp.exp2(tops[k] - new)
                        tops[k], accs[k] = new, add
                for k in range(wide):
                    if h < PARTS - 1:
                        lanes = slice((c * wide + k) * LANES, (c * wide + k + 1) * LANES)
                        col_m[:, lanes], col_p[:, lanes] = tops[k], accs[k]
                    else:
                        full = jnp.max(tops[k], axis=0, keepdims=True)
                        tot = jnp.sum(accs[k] * jnp.exp2(tops[k] - full), axis=0, keepdims=True)
                        b_loc[step, c, k : k + 1, :] = full + jnp.log2(tot)
                if h == PARTS - 1:
                    for o, k in row_peers:
                        copy(
                            b_loc.at[step, c], b_all.at[step, c, row],
                            s_b.at[step], r_b.at[step, c], row_peer(o, k),
                        ).start()

    def receive_b(step, c):
        b_all[step, c, row] = b_loc[step, c]
        got = b_all.at[step, c, 0 : NR - 1]
        copy(got, got, s_b.at[step], r_b.at[step, c], peers[0]).wait_recv()
        pot = math.log2(n_src_total) - lse2([b_all[step, c, i] for i in range(NR)])
        part = slice(c * (ntb // PARTS), (c + 1) * (ntb // PARTS))
        gpot[part, :] = pot
        if step == ITERS - 1:
            g_out[part, :] = (pot + ny[part, :]) * UNSCALE

    first_row_pass()
    build_map_operand()
    for step in range(ITERS):
        if step > 0:
            later_row_pass(step)
        col_pass(step)
    for c in range(PARTS):
        receive_b(ITERS - 1, c)

    half = d // 2
    tail = half + 8
    order = sorted(range(NZ), key=lambda o: -hops(o, NZ))
    tops_of = [None] * NZ
    partner = col_peer(0, 1)

    def weights(t):
        base = pl.multiple_of((z + order[t]) % NZ * LANES, LANES)
        tops = []
        for q in range(LANES // 16):
            rows = pl.ds(pl.multiple_of(base + q * 16, 16), 16)
            ts = [
                score[rows, k * LANES : (k + 1) * LANES] + gpot[k : k + 1, :] for k in range(ntb)
            ]
            top = jnp.max(tree(jnp.maximum, ts), axis=1, keepdims=True)
            for k, v in enumerate(ts):
                w = jnp.exp2(v - top)
                w1 = w.astype(jnp.bfloat16)
                lanes = slice(k * LANES, (k + 1) * LANES)
                wbuf[t % 2, q * 16 : (q + 1) * 16, lanes] = w1
                wbuf[t % 2, LANES + q * 16 : LANES + (q + 1) * 16, lanes] = (
                    w - w1.astype(jnp.float32)
                ).astype(jnp.bfloat16)
            tops.append(jnp.broadcast_to(top, (16, LANES)))
        tops_of[t] = jnp.concatenate(tops, axis=0)

    def pair_copy(t):
        return copy(c_give.at[t], c_pair.at[t], s_p.at[0], r_p.at[t], partner)

    def product(t):
        both = jnp.dot(wbuf[t % 2], yt[...], preferred_element_type=jnp.float32)
        res = both[:LANES] + both[LANES:]
        lo = res[:, :LANES].T
        hi = jnp.where(lane == d + 1, tops_of[t], res[:, LANES:]).T
        num = lo[:d] + lo[d:] + hi[:d]
        c_mine[t, 0:half, :] = jnp.where(core == 0, num[:half], num[half:])
        c_give[t, 0:half, :] = jnp.where(core == 0, num[half:], num[:half])
        c_mine[t, half:tail, :] = hi[d : d + 8]
        c_give[t, half:tail, :] = hi[d : d + 8]
        pair_copy(t).start()

    def merge(parts):
        tops = [p[half + 1 : half + 2, :] for p in parts]
        top = tree(jnp.maximum, tops)
        tot = tree(jnp.add, [p[: half + 1, :] * jnp.exp2(v - top) for p, v in zip(parts, tops)])
        return tot, top

    def pair_merge(t):
        pair_copy(t).wait_recv()
        mine, other = c_mine[t], c_pair[t]
        tot, top = merge([jnp.where(core == 0, mine, other), jnp.where(core == 0, other, mine)])
        rest = jnp.broadcast_to(top, (7, LANES))
        if order[t] == 0:
            c_in[z, 0 : half + 1, :] = tot
            c_in[z, half + 1 : tail, :] = rest
        else:
            c_sum[t, 0 : half + 1, :] = tot
            c_sum[t, half + 1 : tail, :] = rest
            copy(c_sum.at[t], c_in.at[z], s_c.at[0], r_c.at[0], col_peer(order[t], 0)).start()

    weights(0)
    for t in range(NZ):
        if t + 1 < NZ:
            weights(t + 1)
        product(t)
        if t > 1:
            pair_merge(t - 2)
    pair_merge(NZ - 2)
    pair_merge(NZ - 1)
    got = c_in.at[0 : NZ - 1]
    c_whole = copy(got, got, s_c.at[0], r_c.at[0], peers[0])
    c_whole.wait_recv()
    tot, _ = merge([c_in[i] for i in range(NZ)])
    c_res[...] = tot[:half] / tot[half : half + 1]

    def gather_copy(o, k):
        return copy(c_res, c_all.at[core, z], s_g.at[0], r_g.at[o, k], col_peer(o, k))

    def relay_copy(o):
        piece = c_all.at[core, (z + NZ - o) % NZ]
        return copy(piece, piece, s_g.at[0], r_g.at[o, 1], partner)

    direct = NZ // 2
    for o in order[:-1]:
        gather_copy(o, 0).start()
        if o == direct:
            gather_copy(o, 1).start()
    gather_copy(0, 1).start()
    c_all[core, z] = c_res[...]
    for o in order[::-1][1:-1]:
        gather_copy(o, 0).wait_recv()
        relay_copy(o).start()

    for step in range(ITERS):
        a_got, b_got = a_all.at[step, :, 0 : NC - 1], b_all.at[step, :, 0 : NR - 1]
        copy(a_got, a_got, s_a.at[step], r_a.at[step, 0], peers[0]).wait_send()
        copy(b_got, b_got, s_b.at[step], r_b.at[step, 0], peers[0]).wait_send()
    copy(c_give, c_give, s_p.at[0], r_p.at[0], partner).wait_send()
    c_whole.wait_send()
    gather_copy(direct, 0).wait_recv()
    for o in range(NZ):
        gather_copy(o, 1).wait_recv()
    for k in range(2):
        for i in range(NZ):
            m_out[k * half : (k + 1) * half, i * LANES : (i + 1) * LANES] = c_all[k, i]
    flat = c_all.at[0, 0 : NZ - 1]
    copy(c_all.at[0], c_all.at[0], s_g.at[0], r_g.at[0, 0], partner).wait_send()
    copy(flat, flat, s_g.at[0], r_g.at[0, 0], partner).wait_send()


def solution(mesh):
    nrow, ncol = mesh.shape["row"], mesh.shape["col"]

    def shards(source, target):
        d, ns = source.shape
        nt = target.shape[1]
        nsb, ntb = ns // LANES, nt // LANES
        half = d // 2
        f32, bf16 = jnp.float32, jnp.bfloat16
        vmem = pltpu.VMEM
        dma = pltpu.SemaphoreType.DMA
        f, g, m = pl.pallas_call(
            functools.partial(kernel, ns * nrow, nt * ncol),
            out_shape=(
                jax.ShapeDtypeStruct((nsb, LANES), f32),
                jax.ShapeDtypeStruct((ntb, LANES), f32),
                jax.ShapeDtypeStruct((d, ns), f32),
            ),
            in_specs=[pl.BlockSpec(memory_space=pltpu.HBM)] * 2,
            out_specs=(pl.BlockSpec(memory_space=vmem),) * 3,
            scratch_shapes=[
                vmem((d, ns), f32),
                vmem((d, nt), f32),
                vmem((ns, 6 * d), bf16),
                vmem((6 * d, nt), bf16),
                vmem((nt, 2 * LANES), bf16),
                vmem((ns, nt), f32),
                vmem((nsb, LANES), f32),
                vmem((ntb, LANES), f32),
                vmem((ntb, LANES), f32),
                vmem((ns, LANES), f32),
                vmem((ns, LANES), f32),
                vmem((ns, LANES), f32),
                vmem((8, nt), f32),
                vmem((8, nt), f32),
                vmem((ITERS, PARTS, nsb // PARTS, LANES), f32),
                vmem((ITERS, PARTS, NC, nsb // PARTS, LANES), f32),
                vmem((ITERS, PARTS, ntb // PARTS, LANES), f32),
                vmem((ITERS, PARTS, NR, ntb // PARTS, LANES), f32),
                vmem((2, 2 * LANES, nt), bf16),
                vmem((NZ, half + 8, LANES), f32),
                vmem((NZ, half + 8, LANES), f32),
                vmem((NZ, half + 8, LANES), f32),
                vmem((NZ, half + 8, LANES), f32),
                vmem((NZ, half + 8, LANES), f32),
                vmem((half, LANES), f32),
                vmem((2, NZ, half, LANES), f32),
                dma((2,)),
                dma((ITERS,)),
                dma((ITERS, PARTS)),
                dma((ITERS,)),
                dma((ITERS, PARTS)),
                dma((1,)),
                dma((NZ,)),
                dma((1,)),
                dma((1,)),
                dma((1,)),
                dma((NZ, 2)),
            ],
            compiler_params=pltpu.CompilerParams(
                collective_id=0, has_side_effects=True, vmem_limit_bytes=40 * 2**20
            ),
            name="sinkhorn",
        )(source, target)
        return f.reshape(ns), g.reshape(nt), m

    return jax.shard_map(
        shards,
        mesh=mesh,
        in_specs=(P(None, "row"), P(None, "col")),
        out_specs=(P("row"), P("col"), P(None, "row")),
        check_vma=False,
    )
```

time: 76.6 us -> 71.9 us (0.939)
  Pallas kernels: 71.9 us -> 67.2 us
    pallas_call x1, Pallas kernels: 71.9 us -> 67.2 us  [shards(): pl.pallas_call(functools.partial(kernel, ns * nrow, nt * ncol), out_shape...]
where the time goes in v3:
time: 71.9 us; the launch traced here: 71.7 us
  Pallas kernels  67.2 us (93%)
  local copies, waits for them, and re-layouts  3.88 us (5%)
    pallas_call x1, Pallas kernels, shards(): pl.pallas_call(functools.partial(kernel, ns * nrow, nt * ncol), out_shape...  67.2 us
    unnamed x7, local copies, waits for them, and re-layouts  3.88 us

profile of v3, /device:TPU:1, one launch (start us, length us, event | category | flops | bytes accessed | tf_op | source)
XLA Modules:
  0.0 71.7 jit_solution(2533001822117909382)
XLA Ops:
  0.6 0.0 copy-start
  0.6 1.0 %copy-done = f32[64,2048]{1,0:T(8,128)S(1)} copy-done((f32[64,2048]{1,0:T(8,128)S(1)}, f32[64,2048]{1,0:T(8,128)}, u32[]{:S(2)}) %copy-start) | copy-done | bytes 524312
  1.7 0.0 copy-start.1
  1.7 0.9 %copy-done.1 = f32[64,1024]{1,0:T(8,128)S(1)} copy-done((f32[64,1024]{1,0:T(8,128)S(1)}, f32[64,1024]{1,0:T(8,128)}, u32[]{:S(2)}) %copy-start.1) | copy-done | bytes 262168
  2.6 67.2 %sinkhorn.1 = (f32[8,128]{1,0:T(8,128)S(1)}, f32[16,128]{1,0:T(8,128)S(1)}, f32[64,1024]{1,0:T(8,128)S(1)}) custom-call(f32[64,1024]{1,0:T(8,128)S(1)} %copy-done.1, f32[64,2048]{1,0:T(8,128)S(1)} %copy-done), custom_call_target="tpu_custom_call" | custom-call | tf_op jit(solution)/shard_map/sinkhorn/pallas_call | solution.py:437
  69.8 0.6 copy.8
  70.4 0.6 copy.9
  71.0 0.7 copy.10
Async XLA Ops:
  0.6 1.0 %copy-start = (f32[64,2048]{1,0:T(8,128)S(1)}, f32[64,2048]{1,0:T(8,128)}, u32[]{:S(2)}) copy-start(f32[64,2048]{1,0:T(8,128)} %tgt_hbm.1) | copy-start | bytes 1572868
  1.7 0.9 %copy-start.1 = (f32[64,1024]{1,0:T(8,128)S(1)}, f32[64,1024]{1,0:T(8,128)}, u32[]{:S(2)}) copy-start(f32[64,1024]{1,0:T(8,128)} %src_hbm.1) | copy-start | bytes 786436

commit v4 on v3

--- a/solution.py
+++ b/solution.py
@@ -16,6 +16,7 @@
 LANES = 128
 NZ, NX, NY = 8, 4, 8
 NC, NR = 2 * NZ, NX * NY
+VMEM_GRANT = 56_150_000
 PARTS = 2
 
 
@@ -61,9 +62,14 @@
     xk,
     yk,
     yt,
+    yv,
     score,
+    plan,
+    halves,
+    m_acc,
     nx,
     ny,
+    fpot,
     gpot,
     fcol,
     part_m,
@@ -74,7 +80,6 @@
     a_all,
     b_loc,
     b_all,
-    wbuf,
     c_mine,
     c_give,
     c_pair,
@@ -160,15 +165,9 @@
     def build_map_operand():
         for b in range(ntb):
             blk = tgt[:, b * LANES : (b + 1) * LANES]
-            both = jnp.concatenate([blk, blk], axis=0).T
-            t1 = both.astype(jnp.bfloat16).astype(jnp.float32)
-            r = both - t1
-            t2 = r.astype(jnp.bfloat16).astype(jnp.float32)
-            rows = pl.ds(b * LANES, LANES)
-            yt[rows, 0:128] = jnp.where(first, t1, t2).astype(jnp.bfloat16)
-            yt[rows, 128:256] = jnp.where(
-                first, r - t2, jnp.where(lane == d, 1.0, 0.0)
-            ).astype(jnp.bfloat16)
+            yt[b * LANES : (b + 1) * LANES, :] = jnp.concatenate(
+                [blk, jnp.ones((LANES - d, LANES), jnp.float32)], axis=0
+            ).T
 
     def score_tiles(c):
         rows = slice(c * 256, (c + 1) * 256)
@@ -182,27 +181,36 @@
 
             yield tile
 
-    def row_group(base, size, lo, hi, carry):
+    def row_group(base, size):
         rows = pl.ds(base, size)
-        ts = [score[rows, k * LANES : (k + 1) * LANES] + gpot[k : k + 1, :] for k in range(lo, hi)]
+        ts = [score[rows, k * LANES : (k + 1) * LANES] + gpot[k : k + 1, :] for k in range(ntb)]
         top = tree(jnp.maximum, ts)
-        if carry:
-            old = part_m[rows, :]
-            top = jnp.maximum(top, old)
-        tot = tree(jnp.add, [jnp.exp2(t - top) for t in ts])
-        if carry:
-            tot += part_p[rows, :] * jnp.exp2(old - top)
         part_m[rows, :] = top
-        part_p[rows, :] = tot
+        part_p[rows, :] = tree(jnp.add, [jnp.exp2(t - top) for t in ts])
+
+    def plan_group(base, size, lo, hi):
+        rows = pl.ds(base, size)
+        pot = fcol[rows, :]
+        ps = []
+        for k in range(lo, hi):
+            lanes = slice(k * LANES, (k + 1) * LANES)
+            p = jnp.exp2((score[rows, lanes] + pot) + gpot[k : k + 1, :])
+            plan[rows, lanes] = p
+            ps.append(p)
+        tot = tree(jnp.add, ps)
+        part_p[rows, :] = tot if lo == 0 else tot + part_p[rows, :]
 
     def send_rows(step, c):
         for i in range(nsb // PARTS):
             b = c * (nsb // PARTS) + i
-            mt = part_m[b * LANES : (b + 1) * LANES, :].T
             pt = part_p[b * LANES : (b + 1) * LANES, :].T
-            top = jnp.max(mt, axis=0, keepdims=True)
-            tot = jnp.sum(pt * jnp.exp2(mt - top), axis=0, keepdims=True)
-            a_loc[step, c, i : i + 1, :] = top + jnp.log2(tot)
+            if step == 0:
+                mt = part_m[b * LANES : (b + 1) * LANES, :].T
+                top = jnp.max(mt, axis=0, keepdims=True)
+                tot = jnp.sum(pt * jnp.exp2(mt - top), axis=0, keepdims=True)
+                a_loc[step, c, i : i + 1, :] = top + jnp.log2(tot)
+            else:
+                a_loc[step, c, i : i + 1, :] = jnp.sum(pt, axis=0, keepdims=True)
         if step == 0 and c == 0:
             pl.semaphore_wait(barrier, len(peers))
         for o, k in col_peers:
@@ -219,7 +227,7 @@
                 tile()
                 if c > 0:
                     for q in range(2):
-                        row_group((c - 1) * 256 + n * 32 + q * 16, 16, 0, ntb, False)
+                        row_group((c - 1) * 256 + n * 32 + q * 16, 16)
             if c > 0 and c % (count // PARTS) == 0:
                 send_rows(0, c // (count // PARTS) - 1)
 
@@ -232,7 +240,7 @@
 
                 def group(q, _):
                     base = pl.multiple_of(h * size + q * 32, 32)
-                    row_group(base, 32, c * wide, (c + 1) * wide, c > 0)
+                    plan_group(base, 32, c * wide, (c + 1) * wide)
                     return 0
 
                 lax.fori_loop(0, size // 32, group, 0, unroll=8)
@@ -243,16 +251,20 @@
         a_all[step, c, col] = a_loc[step, c]
         got = a_all.at[step, c, 0 : NC - 1]
         copy(got, got, s_a.at[step], r_a.at[step, c], peers[0]).wait_recv()
-        pot = math.log2(n_tgt_total) - lse2([a_all[step, c, i] for i in range(NC)])
         size = nsb // PARTS
+        part = slice(c * size, (c + 1) * size)
+        if step == 0:
+            pot = math.log2(n_tgt_total) - lse2([a_all[step, c, i] for i in range(NC)])
+            fpot[part, :] = pot
+        else:
+            tot = tree(jnp.add, [a_all[step, c, i] for i in range(NC)])
+            pot = (n_tgt_total / n_src_total) / tot
+            f_out[part, :] = (fpot[part, :] + jnp.log2(pot) + nx[part, :]) * UNSCALE
         for i in range(size):
             b = c * size + i
             fcol[b * LANES : (b + 1) * LANES, :] = jnp.broadcast_to(
                 pot[i : i + 1, :], (LANES, LANES)
             ).T
-        if step == ITERS - 1:
-            part = slice(c * size, (c + 1) * size)
-            f_out[part, :] = (pot + nx[part, :]) * UNSCALE
 
     def col_pass(step):
         wide = ntb // PARTS
@@ -268,14 +280,12 @@
                 for b in range(size // 64):
                     for k in range(wide):
                         lanes = slice((c * wide + k) * LANES, (c * wide + k + 1) * LANES)
-                        ts = []
-                        for i in range(8):
-                            at = h * size + b * 64 + i * 8
-                            ts.append(score[at : at + 8, lanes] + fcol[at : at + 8, :])
-                        new = tree(jnp.maximum, ts)
+                        rows = slice(h * size + b * 64, h * size + (b + 1) * 64)
+                        ts = (score[rows, lanes] + fcol[rows, :]).reshape(8, 8, LANES)
+                        new = jnp.max(ts, axis=0)
                         if tops[k] is not None:
                             new = jnp.maximum(new, tops[k])
-                        add = tree(jnp.add, [jnp.exp2(t - new) for t in ts])
+                        add = jnp.sum(jnp.exp2(ts - new[None]), axis=0)
                         if tops[k] is not None:
                             add += accs[k] * jnp.exp2(tops[k] - new)
                         tops[k], accs[k] = new, add
@@ -288,104 +298,126 @@
                         tot = jnp.sum(accs[k] * jnp.exp2(tops[k] - full), axis=0, keepdims=True)
                         b_loc[step, c, k : k + 1, :] = full + jnp.log2(tot)
                 if h == PARTS - 1:
-                    for o, k in row_peers:
-                        copy(
-                            b_loc.at[step, c], b_all.at[step, c, row],
-                            s_b.at[step], r_b.at[step, c], row_peer(o, k),
-                        ).start()
+                    send_cols(step, c)
+
+    def plan_col_pass(step):
+        wide = ntb // PARTS
+        size = ns // PARTS
+        for h in range(PARTS):
+            receive_a(step, h)
+            for c in range(PARTS):
+                accs = [None] * wide
+                for b in range(size // 64):
+                    rows = slice(h * size + b * 64, h * size + (b + 1) * 64)
+                    for k in range(wide):
+                        lanes = slice((c * wide + k) * LANES, (c * wide + k + 1) * LANES)
+                        ps = (plan[rows, lanes] * fcol[rows, :]).reshape(8, 8, LANES)
+                        add = jnp.sum(ps, axis=0)
+                        accs[k] = add if accs[k] is None else accs[k] + add
+                for k in range(wide):
+                    lanes = slice((c * wide + k) * LANES, (c * wide + k + 1) * LANES)
+                    if h > 0:
+                        accs[k] += col_p[:, lanes]
+                    if h < PARTS - 1:
+                        col_p[:, lanes] = accs[k]
+                    else:
+                        b_loc[step, c, k : k + 1, :] = jnp.sum(accs[k], axis=0, keepdims=True)
+                if h == PARTS - 1:
+                    send_cols(step, c)
+
+    def send_cols(step, c):
+        for o, k in row_peers:
+            copy(
+                b_loc.at[step, c], b_all.at[step, c, row],
+                s_b.at[step], r_b.at[step, c], row_peer(o, k),
+            ).start()
 
     def receive_b(step, c):
         b_all[step, c, row] = b_loc[step, c]
         got = b_all.at[step, c, 0 : NR - 1]
         copy(got, got, s_b.at[step], r_b.at[step, c], peers[0]).wait_recv()
-        pot = math.log2(n_src_total) - lse2([b_all[step, c, i] for i in range(NR)])
         part = slice(c * (ntb // PARTS), (c + 1) * (ntb // PARTS))
-        gpot[part, :] = pot
-        if step == ITERS - 1:
-            g_out[part, :] = (pot + ny[part, :]) * UNSCALE
+        if step == 0:
+            gpot[part, :] = -lse2([b_all[step, c, i] for i in range(NR)])
+        else:
+            fac = 1.0 / tree(jnp.add, [b_all[step, c, i] for i in range(NR)])
+            g_out[part, :] = (
+                gpot[part, :] + (jnp.log2(fac) + math.log2(n_src_total)) + ny[part, :]
+            ) * UNSCALE
+            for i in range(ntb // PARTS):
+                b = c * (ntb // PARTS) + i
+                rows = slice(b * LANES, (b + 1) * LANES)
+                val = yt[rows, :] * jnp.broadcast_to(fac[i : i + 1, :], (LANES, LANES)).T
+                v1 = val.astype(jnp.bfloat16)
+                yv[rows, 0:LANES] = v1
+                yv[rows, LANES : 2 * LANES] = (val - v1.astype(jnp.float32)).astype(jnp.bfloat16)
+
+    order = sorted(range(NZ), key=lambda o: -hops(o, NZ))
+
+    def split_plan():
+        for t in range(NZ):
+            base = pl.multiple_of((z + order[t]) % NZ * LANES, LANES)
+            for q in range(LANES // 16):
+                p = plan[pl.ds(pl.multiple_of(base + q * 16, 16), 16), :]
+                p1 = p.astype(jnp.bfloat16)
+                halves[t, q * 16 : (q + 1) * 16, :] = p1
+                halves[t, LANES + q * 16 : LANES + (q + 1) * 16, :] = (
+                    p - p1.astype(jnp.float32)
+                ).astype(jnp.bfloat16)
 
     first_row_pass()
     build_map_operand()
-    for step in range(ITERS):
-        if step > 0:
-            later_row_pass(step)
-        col_pass(step)
-    for c in range(PARTS):
-        receive_b(ITERS - 1, c)
+    col_pass(0)
+    later_row_pass(1)
+    plan_col_pass(1)
+    split_plan()
 
     half = d // 2
-    tail = half + 8
-    order = sorted(range(NZ), key=lambda o: -hops(o, NZ))
-    tops_of = [None] * NZ
     partner = col_peer(0, 1)
 
-    def weights(t):
-        base = pl.multiple_of((z + order[t]) % NZ * LANES, LANES)
-        tops = []
-        for q in range(LANES // 16):
-            rows = pl.ds(pl.multiple_of(base + q * 16, 16), 16)
-            ts = [
-                score[rows, k * LANES : (k + 1) * LANES] + gpot[k : k + 1, :] for k in range(ntb)
-            ]
-            top = jnp.max(tree(jnp.maximum, ts), axis=1, keepdims=True)
-            for k, v in enumerate(ts):
-                w = jnp.exp2(v - top)
-                w1 = w.astype(jnp.bfloat16)
-                lanes = slice(k * LANES, (k + 1) * LANES)
-                wbuf[t % 2, q * 16 : (q + 1) * 16, lanes] = w1
-                wbuf[t % 2, LANES + q * 16 : LANES + (q + 1) * 16, lanes] = (
-                    w - w1.astype(jnp.float32)
-                ).astype(jnp.bfloat16)
-            tops.append(jnp.broadcast_to(top, (16, LANES)))
-        tops_of[t] = jnp.concatenate(tops, axis=0)
+    def product(t, c):
+        part = slice(c * (nt // PARTS), (c + 1) * (nt // PARTS))
+        both = jnp.dot(halves[t, :, part], yv[part, :], preferred_element_type=jnp.float32)
+        both = both[:LANES] + both[LANES:]
+        return both[:, :LANES] + both[:, LANES:]
+
+    for c in range(PARTS - 1):
+        receive_b(1, c)
+        for t in range(NZ):
+            res = product(t, c)
+            m_acc[t] = res if c == 0 else m_acc[t] + res
+    receive_b(1, PARTS - 1)
 
     def pair_copy(t):
         return copy(c_give.at[t], c_pair.at[t], s_p.at[0], r_p.at[t], partner)
 
-    def product(t):
-        both = jnp.dot(wbuf[t % 2], yt[...], preferred_element_type=jnp.float32)
-        res = both[:LANES] + both[LANES:]
-        lo = res[:, :LANES].T
-        hi = jnp.where(lane == d + 1, tops_of[t], res[:, LANES:]).T
-        num = lo[:d] + lo[d:] + hi[:d]
-        c_mine[t, 0:half, :] = jnp.where(core == 0, num[:half], num[half:])
-        c_give[t, 0:half, :] = jnp.where(core == 0, num[half:], num[:half])
-        c_mine[t, half:tail, :] = hi[d : d + 8]
-        c_give[t, half:tail, :] = hi[d : d + 8]
+    def finish_block(t):
+        res = (m_acc[t] + product(t, PARTS - 1)).T
+        c_mine[t, 0:half, :] = jnp.where(core == 0, res[:half], res[half:d])
+        c_give[t, 0:half, :] = jnp.where(core == 0, res[half:d], res[:half])
+        c_mine[t, half : half + 1, :] = res[d : d + 1]
+        c_give[t, half : half + 1, :] = res[d : d + 1]
         pair_copy(t).start()
-
-    def merge(parts):
-        tops = [p[half + 1 : half + 2, :] for p in parts]
-        top = tree(jnp.maximum, tops)
-        tot = tree(jnp.add, [p[: half + 1, :] * jnp.exp2(v - top) for p, v in zip(parts, tops)])
-        return tot, top
 
     def pair_merge(t):
         pair_copy(t).wait_recv()
-        mine, other = c_mine[t], c_pair[t]
-        tot, top = merge([jnp.where(core == 0, mine, other), jnp.where(core == 0, other, mine)])
-        rest = jnp.broadcast_to(top, (7, LANES))
         if order[t] == 0:
-            c_in[z, 0 : half + 1, :] = tot
-            c_in[z, half + 1 : tail, :] = rest
+            c_in[z] = c_mine[t] + c_pair[t]
         else:
-            c_sum[t, 0 : half + 1, :] = tot
-            c_sum[t, half + 1 : tail, :] = rest
+            c_sum[t] = c_mine[t] + c_pair[t]
             copy(c_sum.at[t], c_in.at[z], s_c.at[0], r_c.at[0], col_peer(order[t], 0)).start()
 
-    weights(0)
+    lag = 4
     for t in range(NZ):
-        if t + 1 < NZ:
-            weights(t + 1)
-        product(t)
-        if t > 1:
-            pair_merge(t - 2)
-    pair_merge(NZ - 2)
-    pair_merge(NZ - 1)
+        finish_block(t)
+        if t >= lag:
+            pair_merge(t - lag)
+    for t in range(NZ - lag, NZ):
+        pair_merge(t)
     got = c_in.at[0 : NZ - 1]
     c_whole = copy(got, got, s_c.at[0], r_c.at[0], peers[0])
     c_whole.wait_recv()
-    tot, _ = merge([c_in[i] for i in range(NZ)])
+    tot = tree(jnp.add, [c_in[i] for i in range(NZ)])
     c_res[...] = tot[:half] / tot[half : half + 1]
 
     def gather_copy(o, k):
@@ -421,6 +453,17 @@
     flat = c_all.at[0, 0 : NZ - 1]
     copy(c_all.at[0], c_all.at[0], s_g.at[0], r_g.at[0, 0], partner).wait_send()
     copy(flat, flat, s_g.at[0], r_g.at[0, 0], partner).wait_send()
+
+
+def write_kernel(f, g, m, f_out, g_out, m_out, sems):
+    copies = [
+        pltpu.make_async_copy(a, b, sems.at[i])
+        for i, (a, b) in enumerate(((m, m_out), (g, g_out), (f, f_out)))
+    ]
+    for c in copies:
+        c.start()
+    for c in copies:
+        c.wait()
 
 
 def solution(mesh):
@@ -448,10 +491,15 @@
                 vmem((d, nt), f32),
                 vmem((ns, 6 * d), bf16),
                 vmem((6 * d, nt), bf16),
+                vmem((nt, LANES), f32),
                 vmem((nt, 2 * LANES), bf16),
                 vmem((ns, nt), f32),
+                vmem((ns, nt), f32),
+                vmem((NZ, 2 * LANES, nt), bf16),
+                vmem((NZ, LANES, LANES), f32),
                 vmem((nsb, LANES), f32),
                 vmem((ntb, LANES), f32),
+                vmem((nsb, LANES), f32),
                 vmem((ntb, LANES), f32),
                 vmem((ns, LANES), f32),
                 vmem((ns, LANES), f32),
@@ -462,12 +510,11 @@
                 vmem((ITERS, PARTS, NC, nsb // PARTS, LANES), f32),
                 vmem((ITERS, PARTS, ntb // PARTS, LANES), f32),
                 vmem((ITERS, PARTS, NR, ntb // PARTS, LANES), f32),
-                vmem((2, 2 * LANES, nt), bf16),
-                vmem((NZ, half + 8, LANES), f32),
-                vmem((NZ, half + 8, LANES), f32),
-                vmem((NZ, half + 8, LANES), f32),
-                vmem((NZ, half + 8, LANES), f32),
-                vmem((NZ, half + 8, LANES), f32),
+                vmem((NZ, half + 1, LANES), f32),
+                vmem((NZ, half + 1, LANES), f32),
+                vmem((NZ, half + 1, LANES), f32),
+                vmem((NZ, half + 1, LANES), f32),
+                vmem((NZ, half + 1, LANES), f32),
                 vmem((half, LANES), f32),
                 vmem((2, NZ, half, LANES), f32),
                 dma((2,)),
@@ -483,10 +530,23 @@
                 dma((NZ, 2)),
             ],
             compiler_params=pltpu.CompilerParams(
-                collective_id=0, has_side_effects=True, vmem_limit_bytes=40 * 2**20
+                collective_id=0, has_side_effects=True, vmem_limit_bytes=VMEM_GRANT
             ),
             name="sinkhorn",
         )(source, target)
+        f, g, m = pl.pallas_call(
+            write_kernel,
+            out_shape=(
+                jax.ShapeDtypeStruct((nsb, LANES), f32),
+                jax.ShapeDtypeStruct((ntb, LANES), f32),
+                jax.ShapeDtypeStruct((d, ns), f32),
+            ),
+            in_specs=[pl.BlockSpec(memory_space=pl.ANY)] * 3,
+            out_specs=(pl.BlockSpec(memory_space=pl.ANY),) * 3,
+            scratch_shapes=[dma((3,))],
+            compiler_params=pltpu.CompilerParams(vmem_limit_bytes=2**20),
+            name="write_results",
+        )(f, g, m)
         return f.reshape(ns), g.reshape(nt), m
 
     return jax.shard_map(

time: 71.9 us -> 65.3 us (0.908)
  local copies, waits for them, and re-layouts: 3.88 us -> 0 us
  Pallas kernels: 67.2 us -> 64.4 us
    unnamed x7 -> x0, local copies, waits for them, and re-layouts: 3.88 us -> none
    pallas_call x1, Pallas kernels: 67.2 us -> 63.6 us  [shards(): pl.pallas_call(functools.partial(kernel, ns * nrow, nt * ncol), out_shape...]
    pallas_call x0 -> x1, Pallas kernels: none -> 0.73 us  [shards(): pl.pallas_call(write_kernel, out_shape=(jax.ShapeDtypeStruct((nsb, LANES)...]
where the time goes in v4:
time: 65.3 us; the launch traced here: 65.1 us
  Pallas kernels  64.4 us (99%)
  between operations  0.8 us (1%)
    pallas_call x1, Pallas kernels, shards(): pl.pallas_call(functools.partial(kernel, ns * nrow, nt * ncol), out_shape...  63.6 us

profile of v4, /device:TPU:1, one launch (start us, length us, event | category | flops | bytes accessed | tf_op | source)
XLA Modules:
  0.0 65.1 jit_solution(10961219703333931873)
XLA Ops:
  0.6 63.6 %sinkhorn.1 = (f32[8,128]{1,0:T(8,128)S(1)}, f32[16,128]{1,0:T(8,128)S(1)}, f32[64,1024]{1,0:T(8,128)S(1)}) custom-call(f32[64,1024]{1,0:T(8,128)} %src_hbm.1, f32[64,2048]{1,0:T(8,128)} %tgt_hbm.1), custom_call_target="tpu_custom_call" | custom-call | tf_op jit(solution)/shard_map/sinkhorn/pallas_call | solution.py:480
  64.3 0.7 %write_results.1 = (f32[8,128]{1,0:T(8,128)}, f32[16,128]{1,0:T(8,128)}, f32[64,1024]{1,0:T(8,128)}) custom-call(f32[8,128]{1,0:T(8,128)S(1)} %get-tuple-element.9.f, f32[16,128]{1,0:T(8,128)S(1)} %get-tuple-element.10.g, f32[64,1024]{1,0:T(8,128)S(1)} %get-tuple-element.11.m), custom_call_target="tpu_custom_call" | custom-call | tf_op jit(solution)/shard_map/write_results/pallas_call | solution.py:537

commit v5 on v4

--- a/solution.py
+++ b/solution.py
@@ -122,7 +122,9 @@
     def row_peer(o, k):
         return (((y + o) % NY) * NX + (x + k) % NX, col)
 
-    peers = [col_peer(*p) for p in col_peers] + [row_peer(*p) for p in row_peers]
+    col_ids = {p: col_peer(*p) for p in col_peers}
+    row_ids = {p: row_peer(*p) for p in row_peers}
+    peers = list(col_ids.values()) + list(row_ids.values())
     barrier = pltpu.get_barrier_semaphore()
     for peer in peers:
         pl.semaphore_signal(barrier, inc=1, device_id=peer, device_id_type=MESH)
@@ -329,7 +331,7 @@
         for o, k in row_peers:
             copy(
                 b_loc.at[step, c], b_all.at[step, c, row],
-                s_b.at[step], r_b.at[step, c], row_peer(o, k),
+                s_b.at[step], r_b.at[step, c], row_ids[o, k],
             ).start()
 
     def receive_b(step, c):
@@ -360,8 +362,9 @@
             for q in range(LANES // 16):
                 p = plan[pl.ds(pl.multiple_of(base + q * 16, 16), 16), :]
                 p1 = p.astype(jnp.bfloat16)
-                halves[t, q * 16 : (q + 1) * 16, :] = p1
-                halves[t, LANES + q * 16 : LANES + (q + 1) * 16, :] = (
+                at = t * 2 * LANES + q * 16
+                halves[at : at + 16, :] = p1
+                halves[at + LANES : at + LANES + 16, :] = (
                     p - p1.astype(jnp.float32)
                 ).astype(jnp.bfloat16)
 
@@ -375,45 +378,54 @@
     half = d // 2
     partner = col_peer(0, 1)
 
-    def product(t, c):
+    def product(t, count, c):
         part = slice(c * (nt // PARTS), (c + 1) * (nt // PARTS))
-        both = jnp.dot(halves[t, :, part], yv[part, :], preferred_element_type=jnp.float32)
-        both = both[:LANES] + both[LANES:]
-        return both[:, :LANES] + both[:, LANES:]
+        rows = slice(t * 2 * LANES, (t + count) * 2 * LANES)
+        both = jnp.dot(halves[rows, part], yv[part, :], preferred_element_type=jnp.float32)
+        both = both[:, :LANES] + both[:, LANES:]
+        out = []
+        for i in range(count):
+            at = i * 2 * LANES
+            out.append(both[at : at + LANES] + both[at + LANES : at + 2 * LANES])
+        return out
 
     for c in range(PARTS - 1):
         receive_b(1, c)
-        for t in range(NZ):
-            res = product(t, c)
+        for t, res in enumerate(product(0, NZ, c)):
             m_acc[t] = res if c == 0 else m_acc[t] + res
     receive_b(1, PARTS - 1)
 
-    def pair_copy(t):
-        return copy(c_give.at[t], c_pair.at[t], s_p.at[0], r_p.at[t], partner)
-
-    def finish_block(t):
-        res = (m_acc[t] + product(t, PARTS - 1)).T
-        c_mine[t, 0:half, :] = jnp.where(core == 0, res[:half], res[half:d])
-        c_give[t, 0:half, :] = jnp.where(core == 0, res[half:d], res[:half])
-        c_mine[t, half : half + 1, :] = res[d : d + 1]
-        c_give[t, half : half + 1, :] = res[d : d + 1]
-        pair_copy(t).start()
-
-    def pair_merge(t):
-        pair_copy(t).wait_recv()
-        if order[t] == 0:
-            c_in[z] = c_mine[t] + c_pair[t]
-        else:
-            c_sum[t] = c_mine[t] + c_pair[t]
-            copy(c_sum.at[t], c_in.at[z], s_c.at[0], r_c.at[0], col_peer(order[t], 0)).start()
-
-    lag = 4
-    for t in range(NZ):
-        finish_block(t)
-        if t >= lag:
-            pair_merge(t - lag)
-    for t in range(NZ - lag, NZ):
-        pair_merge(t)
+    GROUP = NZ // 2
+
+    def pair_copy(g):
+        part = pl.ds(g * GROUP, GROUP)
+        return copy(c_give.at[part], c_pair.at[part], s_p.at[0], r_p.at[g], partner)
+
+    def finish_group(g):
+        for i, res in enumerate(product(g * GROUP, GROUP, PARTS - 1)):
+            t = g * GROUP + i
+            res = (m_acc[t] + res).T
+            c_mine[t, 0:half, :] = jnp.where(core == 0, res[:half], res[half:d])
+            c_give[t, 0:half, :] = jnp.where(core == 0, res[half:d], res[:half])
+            c_mine[t, half : half + 1, :] = res[d : d + 1]
+            c_give[t, half : half + 1, :] = res[d : d + 1]
+        pair_copy(g).start()
+
+    def merge_group(g):
+        pair_copy(g).wait_recv()
+        for t in range(g * GROUP, (g + 1) * GROUP):
+            if order[t] == 0:
+                c_in[z] = c_mine[t] + c_pair[t]
+            else:
+                c_sum[t] = c_mine[t] + c_pair[t]
+        for t in range(g * GROUP, (g + 1) * GROUP):
+            if order[t] != 0:
+                copy(c_sum.at[t], c_in.at[z], s_c.at[0], r_c.at[0], col_peer(order[t], 0)).start()
+
+    finish_group(0)
+    finish_group(1)
+    merge_group(0)
+    merge_group(1)
     got = c_in.at[0 : NZ - 1]
     c_whole = copy(got, got, s_c.at[0], r_c.at[0], peers[0])
     c_whole.wait_recv()
@@ -495,7 +507,7 @@
                 vmem((nt, 2 * LANES), bf16),
                 vmem((ns, nt), f32),
                 vmem((ns, nt), f32),
-                vmem((NZ, 2 * LANES, nt), bf16),
+                vmem((NZ * 2 * LANES, nt), bf16),
                 vmem((NZ, LANES, LANES), f32),
                 vmem((nsb, LANES), f32),
                 vmem((ntb, LANES), f32),

time: 65.3 us -> 65.5 us (level)
  no operation moved by 1% of the time
where the time goes in v5:
time: 65.5 us; the launch traced here: 65.3 us
  Pallas kernels  64.5 us (98%)
  between operations  0.8 us (1%)
    pallas_call x1, Pallas kernels, shards(): pl.pallas_call(functools.partial(kernel, ns * nrow, nt * ncol), out_shape...  63.8 us

profile of v5, /device:TPU:1, one launch (start us, length us, event | category | flops | bytes accessed | tf_op | source)
XLA Modules:
  0.0 65.3 jit_solution(9874759410475044333)
XLA Ops:
  0.6 63.8 %sinkhorn.1 = (f32[8,128]{1,0:T(8,128)S(1)}, f32[16,128]{1,0:T(8,128)S(1)}, f32[64,1024]{1,0:T(8,128)S(1)}) custom-call(f32[64,1024]{1,0:T(8,128)} %src_hbm.1, f32[64,2048]{1,0:T(8,128)} %tgt_hbm.1), custom_call_target="tpu_custom_call" | custom-call | tf_op jit(solution)/shard_map/sinkhorn/pallas_call | solution.py:492
  64.4 0.7 %write_results.1 = (f32[8,128]{1,0:T(8,128)}, f32[16,128]{1,0:T(8,128)}, f32[64,1024]{1,0:T(8,128)}) custom-call(f32[8,128]{1,0:T(8,128)S(1)} %get-tuple-element.9.f, f32[16,128]{1,0:T(8,128)S(1)} %get-tuple-element.10.g, f32[64,1024]{1,0:T(8,128)S(1)} %get-tuple-element.11.m), custom_call_target="tpu_custom_call" | custom-call | tf_op jit(solution)/shard_map/write_results/pallas_call | solution.py:549

commit v6 on v5

--- a/solution.py
+++ b/solution.py
@@ -15,7 +15,7 @@
 UNSCALE = EPSILON * math.log(2.0)
 LANES = 128
 NZ, NX, NY = 8, 4, 8
-NC, NR = 2 * NZ, NX * NY
+NC = 2 * NZ
 VMEM_GRANT = 56_150_000
 PARTS = 2
 
@@ -79,7 +79,9 @@
     a_loc,
     a_all,
     b_loc,
-    b_all,
+    b_y,
+    b_mid,
+    b_x,
     c_mine,
     c_give,
     c_pair,
@@ -90,8 +92,10 @@
     load,
     s_a,
     r_a,
-    s_b,
-    r_b,
+    s_by,
+    r_by,
+    s_bx,
+    r_bx,
     s_p,
     r_p,
     s_c,
@@ -113,18 +117,22 @@
 
     col_peers = [(o, k) for o in range(NZ) for k in range(2) if (o, k) != (0, 0)]
     col_peers.sort(key=lambda p: -hops(p[0], NZ))
-    row_peers = [(o, k) for o in range(NY) for k in range(NX) if (o, k) != (0, 0)]
-    row_peers.sort(key=lambda p: -hops(p[0], NY) - hops(p[1], NX))
+    y_peers = sorted(range(1, NY), key=lambda o: -hops(o, NY))
+    x_peers = sorted(range(1, NX), key=lambda o: -hops(o, NX))
 
     def col_peer(o, k):
         return (row, ((z + o) % NZ) * 2 + (core + k) % 2)
 
-    def row_peer(o, k):
-        return (((y + o) % NY) * NX + (x + k) % NX, col)
+    def y_peer(o):
+        return (((y + o) % NY) * NX + x, col)
+
+    def x_peer(o):
+        return (y * NX + (x + o) % NX, col)
 
     col_ids = {p: col_peer(*p) for p in col_peers}
-    row_ids = {p: row_peer(*p) for p in row_peers}
-    peers = list(col_ids.values()) + list(row_ids.values())
+    y_ids = [y_peer(o) for o in y_peers]
+    x_ids = [x_peer(o) for o in x_peers]
+    peers = list(col_ids.values()) + y_ids + x_ids
     barrier = pltpu.get_barrier_semaphore()
     for peer in peers:
         pl.semaphore_signal(barrier, inc=1, device_id=peer, device_id_type=MESH)
@@ -328,21 +336,31 @@
                     send_cols(step, c)
 
     def send_cols(step, c):
-        for o, k in row_peers:
+        for peer in y_ids:
             copy(
-                b_loc.at[step, c], b_all.at[step, c, row],
-                s_b.at[step], r_b.at[step, c], row_ids[o, k],
+                b_loc.at[step, c], b_y.at[step, c, y], s_by.at[step], r_by.at[step, c], peer
             ).start()
 
+    def relay_cols(step, c):
+        b_y[step, c, y] = b_loc[step, c]
+        got = b_y.at[step, c, 0 : NY - 1]
+        copy(got, got, s_by.at[step], r_by.at[step, c], peers[0]).wait_recv()
+        parts = [b_y[step, c, i] for i in range(NY)]
+        b_mid[step, c] = lse2(parts) if step == 0 else tree(jnp.add, parts)
+        for peer in x_ids:
+            copy(
+                b_mid.at[step, c], b_x.at[step, c, x], s_bx.at[step], r_bx.at[step, c], peer
+            ).start()
+
     def receive_b(step, c):
-        b_all[step, c, row] = b_loc[step, c]
-        got = b_all.at[step, c, 0 : NR - 1]
-        copy(got, got, s_b.at[step], r_b.at[step, c], peers[0]).wait_recv()
+        b_x[step, c, x] = b_mid[step, c]
+        got = b_x.at[step, c, 0 : NX - 1]
+        copy(got, got, s_bx.at[step], r_bx.at[step, c], peers[0]).wait_recv()
         part = slice(c * (ntb // PARTS), (c + 1) * (ntb // PARTS))
         if step == 0:
-            gpot[part, :] = -lse2([b_all[step, c, i] for i in range(NR)])
+            gpot[part, :] = -lse2([b_x[step, c, i] for i in range(NX)])
         else:
-            fac = 1.0 / tree(jnp.add, [b_all[step, c, i] for i in range(NR)])
+            fac = 1.0 / tree(jnp.add, [b_x[step, c, i] for i in range(NX)])
             g_out[part, :] = (
                 gpot[part, :] + (jnp.log2(fac) + math.log2(n_src_total)) + ny[part, :]
             ) * UNSCALE
@@ -371,9 +389,13 @@
     first_row_pass()
     build_map_operand()
     col_pass(0)
+    for c in range(PARTS):
+        relay_cols(0, c)
     later_row_pass(1)
     plan_col_pass(1)
     split_plan()
+    for c in range(PARTS):
+        relay_cols(1, c)
 
     half = d // 2
     partner = col_peer(0, 1)
@@ -395,7 +417,7 @@
             m_acc[t] = res if c == 0 else m_acc[t] + res
     receive_b(1, PARTS - 1)
 
-    GROUP = NZ // 2
+    GROUP = 2
 
     def pair_copy(g):
         part = pl.ds(g * GROUP, GROUP)
@@ -422,10 +444,11 @@
             if order[t] != 0:
                 copy(c_sum.at[t], c_in.at[z], s_c.at[0], r_c.at[0], col_peer(order[t], 0)).start()
 
-    finish_group(0)
-    finish_group(1)
-    merge_group(0)
-    merge_group(1)
+    for g in range(NZ // GROUP):
+        finish_group(g)
+        if g > 0:
+            merge_group(g - 1)
+    merge_group(NZ // GROUP - 1)
     got = c_in.at[0 : NZ - 1]
     c_whole = copy(got, got, s_c.at[0], r_c.at[0], peers[0])
     c_whole.wait_recv()
@@ -451,9 +474,11 @@
         relay_copy(o).start()
 
     for step in range(ITERS):
-        a_got, b_got = a_all.at[step, :, 0 : NC - 1], b_all.at[step, :, 0 : NR - 1]
+        a_got = a_all.at[step, :, 0 : NC - 1]
+        y_got, x_got = b_y.at[step, :, 0 : NY - 1], b_x.at[step, :, 0 : NX - 1]
         copy(a_got, a_got, s_a.at[step], r_a.at[step, 0], peers[0]).wait_send()
-        copy(b_got, b_got, s_b.at[step], r_b.at[step, 0], peers[0]).wait_send()
+        copy(y_got, y_got, s_by.at[step], r_by.at[step, 0], peers[0]).wait_send()
+        copy(x_got, x_got, s_bx.at[step], r_bx.at[step, 0], peers[0]).wait_send()
     copy(c_give, c_give, s_p.at[0], r_p.at[0], partner).wait_send()
     c_whole.wait_send()
     gather_copy(direct, 0).wait_recv()
@@ -521,7 +546,9 @@
                 vmem((ITERS, PARTS, nsb // PARTS, LANES), f32),
                 vmem((ITERS, PARTS, NC, nsb // PARTS, LANES), f32),
                 vmem((ITERS, PARTS, ntb // PARTS, LANES), f32),
-                vmem((ITERS, PARTS, NR, ntb // PARTS, LANES), f32),
+                vmem((ITERS, PARTS, NY, ntb // PARTS, LANES), f32),
+                vmem((ITERS, PARTS, ntb // PARTS, LANES), f32),
+                vmem((ITERS, PARTS, NX, ntb // PARTS, LANES), f32),
                 vmem((NZ, half + 1, LANES), f32),
                 vmem((NZ, half + 1, LANES), f32),
                 vmem((NZ, half + 1, LANES), f32),
@@ -530,6 +557,8 @@
                 vmem((half, LANES), f32),
                 vmem((2, NZ, half, LANES), f32),
                 dma((2,)),
+                dma((ITERS,)),
+                dma((ITERS, PARTS)),
                 dma((ITERS,)),
                 dma((ITERS, PARTS)),
                 dma((ITERS,)),

time: 65.5 us -> 64.2 us (0.980)
  Pallas kernels: 64.5 us -> 63.2 us
    pallas_call x1, Pallas kernels: 63.8 us -> 62.5 us  [shards(): pl.pallas_call(functools.partial(kernel, ns * nrow, nt * ncol), out_shape...]
where the time goes in v6:
time: 64.2 us; the launch traced here: 64 us
  Pallas kernels  63.2 us (98%)
  between operations  0.8 us (1%)
    pallas_call x1, Pallas kernels, shards(): pl.pallas_call(functools.partial(kernel, ns * nrow, nt * ncol), out_shape...  62.5 us

profile of v6, /device:TPU:1, one launch (start us, length us, event | category | flops | bytes accessed | tf_op | source)
XLA Modules:
  0.0 64.0 jit_solution(5443747994909661847)
XLA Ops:
  0.6 62.5 %sinkhorn.1 = (f32[8,128]{1,0:T(8,128)S(1)}, f32[16,128]{1,0:T(8,128)S(1)}, f32[64,1024]{1,0:T(8,128)S(1)}) custom-call(f32[64,1024]{1,0:T(8,128)} %src_hbm.1, f32[64,2048]{1,0:T(8,128)} %tgt_hbm.1), custom_call_target="tpu_custom_call" | custom-call | tf_op jit(solution)/shard_map/sinkhorn/pallas_call | solution.py:517
  63.1 0.7 %write_results.1 = (f32[8,128]{1,0:T(8,128)}, f32[16,128]{1,0:T(8,128)}, f32[64,1024]{1,0:T(8,128)}) custom-call(f32[8,128]{1,0:T(8,128)S(1)} %get-tuple-element.9.f, f32[16,128]{1,0:T(8,128)S(1)} %get-tuple-element.10.g, f32[64,1024]{1,0:T(8,128)S(1)} %get-tuple-element.11.m), custom_call_target="tpu_custom_call" | custom-call | tf_op jit(solution)/shard_map/write_results/pallas_call | solution.py:578

commit v7 on v6

--- a/solution.py
+++ b/solution.py
@@ -17,7 +17,8 @@
 NZ, NX, NY = 8, 4, 8
 NC = 2 * NZ
 VMEM_GRANT = 56_150_000
-PARTS = 2
+ROW_PARTS, COL_PARTS = 4, 2
+GROUP = 2
 
 
 def normalize(points):
@@ -211,8 +212,8 @@
         part_p[rows, :] = tot if lo == 0 else tot + part_p[rows, :]
 
     def send_rows(step, c):
-        for i in range(nsb // PARTS):
-            b = c * (nsb // PARTS) + i
+        for i in range(nsb // ROW_PARTS):
+            b = c * (nsb // ROW_PARTS) + i
             pt = part_p[b * LANES : (b + 1) * LANES, :].T
             if step == 0:
                 mt = part_m[b * LANES : (b + 1) * LANES, :].T
@@ -238,30 +239,31 @@
                 if c > 0:
                     for q in range(2):
                         row_group((c - 1) * 256 + n * 32 + q * 16, 16)
-            if c > 0 and c % (count // PARTS) == 0:
-                send_rows(0, c // (count // PARTS) - 1)
+            if c > 0 and c % (count // ROW_PARTS) == 0:
+                send_rows(0, c // (count // ROW_PARTS) - 1)
 
     def later_row_pass(step):
-        wide = ntb // PARTS
-        for c in range(PARTS):
+        wide = ntb // COL_PARTS
+        tall = 256 // wide
+        for c in range(COL_PARTS):
             receive_b(step - 1, c)
-            size = ns // PARTS
-            for h in range(PARTS):
+            size = ns // ROW_PARTS
+            for h in range(ROW_PARTS):
 
                 def group(q, _):
-                    base = pl.multiple_of(h * size + q * 32, 32)
-                    plan_group(base, 32, c * wide, (c + 1) * wide)
+                    base = pl.multiple_of(h * size + q * tall, tall)
+                    plan_group(base, tall, c * wide, (c + 1) * wide)
                     return 0
 
-                lax.fori_loop(0, size // 32, group, 0, unroll=8)
-                if c == PARTS - 1:
+                lax.fori_loop(0, size // tall, group, 0, unroll=8)
+                if c == COL_PARTS - 1:
                     send_rows(step, h)
 
     def receive_a(step, c):
         a_all[step, c, col] = a_loc[step, c]
         got = a_all.at[step, c, 0 : NC - 1]
         copy(got, got, s_a.at[step], r_a.at[step, c], peers[0]).wait_recv()
-        size = nsb // PARTS
+        size = nsb // ROW_PARTS
         part = slice(c * size, (c + 1) * size)
         if step == 0:
             pot = math.log2(n_tgt_total) - lse2([a_all[step, c, i] for i in range(NC)])
@@ -277,11 +279,12 @@
             ).T
 
     def col_pass(step):
-        wide = ntb // PARTS
-        size = ns // PARTS
-        for h in range(PARTS):
+        wide = 8
+        per = ntb // COL_PARTS // wide
+        size = ns // ROW_PARTS
+        for h in range(ROW_PARTS):
             receive_a(step, h)
-            for c in range(PARTS):
+            for c in range(ntb // wide):
                 tops, accs = [None] * wide, [None] * wide
                 if h > 0:
                     for k in range(wide):
@@ -300,22 +303,23 @@
                             add += accs[k] * jnp.exp2(tops[k] - new)
                         tops[k], accs[k] = new, add
                 for k in range(wide):
-                    if h < PARTS - 1:
+                    if h < ROW_PARTS - 1:
                         lanes = slice((c * wide + k) * LANES, (c * wide + k + 1) * LANES)
                         col_m[:, lanes], col_p[:, lanes] = tops[k], accs[k]
                     else:
                         full = jnp.max(tops[k], axis=0, keepdims=True)
                         tot = jnp.sum(accs[k] * jnp.exp2(tops[k] - full), axis=0, keepdims=True)
-                        b_loc[step, c, k : k + 1, :] = full + jnp.log2(tot)
-                if h == PARTS - 1:
-                    send_cols(step, c)
+                        b_loc[step, c // per, c % per * wide + k : c % per * wide + k + 1, :] = full + jnp.log2(tot)
+                if h == ROW_PARTS - 1 and c % per == per - 1:
+                    send_cols(step, c // per)
 
     def plan_col_pass(step):
-        wide = ntb // PARTS
-        size = ns // PARTS
-        for h in range(PARTS):
+        wide = 8
+        per = ntb // COL_PARTS // wide
+        size = ns // ROW_PARTS
+        for h in range(ROW_PARTS):
             receive_a(step, h)
-            for c in range(PARTS):
+            for c in range(ntb // wide):
                 accs = [None] * wide
                 for b in range(size // 64):
                     rows = slice(h * size + b * 64, h * size + (b + 1) * 64)
@@ -328,12 +332,12 @@
                     lanes = slice((c * wide + k) * LANES, (c * wide + k + 1) * LANES)
                     if h > 0:
                         accs[k] += col_p[:, lanes]
-                    if h < PARTS - 1:
+                    if h < ROW_PARTS - 1:
                         col_p[:, lanes] = accs[k]
                     else:
-                        b_loc[step, c, k : k + 1, :] = jnp.sum(accs[k], axis=0, keepdims=True)
-                if h == PARTS - 1:
-                    send_cols(step, c)
+                        b_loc[step, c // per, c % per * wide + k : c % per * wide + k + 1, :] = jnp.sum(accs[k], axis=0, keepdims=True)
+                if h == ROW_PARTS - 1 and c % per == per - 1:
+                    send_cols(step, c // per)
 
     def send_cols(step, c):
         for peer in y_ids:
@@ -356,7 +360,7 @@
         b_x[step, c, x] = b_mid[step, c]
         got = b_x.at[step, c, 0 : NX - 1]
         copy(got, got, s_bx.at[step], r_bx.at[step, c], peers[0]).wait_recv()
-        part = slice(c * (ntb // PARTS), (c + 1) * (ntb // PARTS))
+        part = slice(c * (ntb // COL_PARTS), (c + 1) * (ntb // COL_PARTS))
         if step == 0:
             gpot[part, :] = -lse2([b_x[step, c, i] for i in range(NX)])
         else:
@@ -364,8 +368,8 @@
             g_out[part, :] = (
                 gpot[part, :] + (jnp.log2(fac) + math.log2(n_src_total)) + ny[part, :]
             ) * UNSCALE
-            for i in range(ntb // PARTS):
-                b = c * (ntb // PARTS) + i
+            for i in range(ntb // COL_PARTS):
+                b = c * (ntb // COL_PARTS) + i
                 rows = slice(b * LANES, (b + 1) * LANES)
                 val = yt[rows, :] * jnp.broadcast_to(fac[i : i + 1, :], (LANES, LANES)).T
                 v1 = val.astype(jnp.bfloat16)
@@ -389,19 +393,19 @@
     first_row_pass()
     build_map_operand()
     col_pass(0)
-    for c in range(PARTS):
+    for c in range(COL_PARTS):
         relay_cols(0, c)
     later_row_pass(1)
     plan_col_pass(1)
     split_plan()
-    for c in range(PARTS):
+    for c in range(COL_PARTS):
         relay_cols(1, c)
 
     half = d // 2
     partner = col_peer(0, 1)
 
     def product(t, count, c):
-        part = slice(c * (nt // PARTS), (c + 1) * (nt // PARTS))
+        part = slice(c * (nt // COL_PARTS), (c + 1) * (nt // COL_PARTS))
         rows = slice(t * 2 * LANES, (t + count) * 2 * LANES)
         both = jnp.dot(halves[rows, part], yv[part, :], preferred_element_type=jnp.float32)
         both = both[:, :LANES] + both[:, LANES:]
@@ -411,22 +415,21 @@
             out.append(both[at : at + LANES] + both[at + LANES : at + 2 * LANES])
         return out
 
-    for c in range(PARTS - 1):
+    for c in range(COL_PARTS - 1):
         receive_b(1, c)
         for t, res in enumerate(product(0, NZ, c)):
             m_acc[t] = res if c == 0 else m_acc[t] + res
-    receive_b(1, PARTS - 1)
-
-    GROUP = 2
+    receive_b(1, COL_PARTS - 1)
+
 
     def pair_copy(g):
         part = pl.ds(g * GROUP, GROUP)
         return copy(c_give.at[part], c_pair.at[part], s_p.at[0], r_p.at[g], partner)
 
     def finish_group(g):
-        for i, res in enumerate(product(g * GROUP, GROUP, PARTS - 1)):
+        for i, res in enumerate(product(g * GROUP, GROUP, COL_PARTS - 1)):
             t = g * GROUP + i
-            res = (m_acc[t] + res).T
+            res = (res if COL_PARTS == 1 else m_acc[t] + res).T
             c_mine[t, 0:half, :] = jnp.where(core == 0, res[:half], res[half:d])
             c_give[t, 0:half, :] = jnp.where(core == 0, res[half:d], res[:half])
             c_mine[t, half : half + 1, :] = res[d : d + 1]
@@ -543,12 +546,12 @@
                 vmem((ns, LANES), f32),
                 vmem((8, nt), f32),
                 vmem((8, nt), f32),
-                vmem((ITERS, PARTS, nsb // PARTS, LANES), f32),
-                vmem((ITERS, PARTS, NC, nsb // PARTS, LANES), f32),
-                vmem((ITERS, PARTS, ntb // PARTS, LANES), f32),
-                vmem((ITERS, PARTS, NY, ntb // PARTS, LANES), f32),
-                vmem((ITERS, PARTS, ntb // PARTS, LANES), f32),
-                vmem((ITERS, PARTS, NX, ntb // PARTS, LANES), f32),
+                vmem((ITERS, ROW_PARTS, nsb // ROW_PARTS, LANES), f32),
+                vmem((ITERS, ROW_PARTS, NC, nsb // ROW_PARTS, LANES), f32),
+                vmem((ITERS, COL_PARTS, ntb // COL_PARTS, LANES), f32),
+                vmem((ITERS, COL_PARTS, NY, ntb // COL_PARTS, LANES), f32),
+                vmem((ITERS, COL_PARTS, ntb // COL_PARTS, LANES), f32),
+                vmem((ITERS, COL_PARTS, NX, ntb // COL_PARTS, LANES), f32),
                 vmem((NZ, half + 1, LANES), f32),
                 vmem((NZ, half + 1, LANES), f32),
                 vmem((NZ, half + 1, LANES), f32),
@@ -558,11 +561,11 @@
                 vmem((2, NZ, half, LANES), f32),
                 dma((2,)),
                 dma((ITERS,)),
-                dma((ITERS, PARTS)),
+                dma((ITERS, ROW_PARTS)),
                 dma((ITERS,)),
-                dma((ITERS, PARTS)),
+                dma((ITERS, COL_PARTS)),
                 dma((ITERS,)),
-                dma((ITERS, PARTS)),
+                dma((ITERS, COL_PARTS)),
                 dma((1,)),
                 dma((NZ,)),
                 dma((1,)),

time: 64.2 us -> 64.7 us (level)
  Pallas kernels: 63.2 us -> 63.9 us
    pallas_call x1, Pallas kernels: 62.5 us -> 63.2 us  [shards(): pl.pallas_call(functools.partial(kernel, ns * nrow, nt * ncol), out_shape...]
where the time goes in v7:
time: 64.7 us; the launch traced here: 64.5 us
  Pallas kernels  63.9 us (99%)
    pallas_call x1, Pallas kernels, shards(): pl.pallas_call(functools.partial(kernel, ns * nrow, nt * ncol), out_shape...  63.2 us

profile of v7, /device:TPU:1, one launch (start us, length us, event | category | flops | bytes accessed | tf_op | source)
XLA Modules:
  0.0 64.5 jit_solution(4650506074642394549)
XLA Ops:
  0.6 63.2 %sinkhorn.1 = (f32[8,128]{1,0:T(8,128)S(1)}, f32[16,128]{1,0:T(8,128)S(1)}, f32[64,1024]{1,0:T(8,128)S(1)}) custom-call(f32[64,1024]{1,0:T(8,128)} %src_hbm.1, f32[64,2048]{1,0:T(8,128)} %tgt_hbm.1), custom_call_target="tpu_custom_call" | custom-call | tf_op jit(solution)/shard_map/sinkhorn/pallas_call | solution.py:520
  63.8 0.7 %write_results.1 = (f32[8,128]{1,0:T(8,128)}, f32[16,128]{1,0:T(8,128)}, f32[64,1024]{1,0:T(8,128)}) custom-call(f32[8,128]{1,0:T(8,128)S(1)} %get-tuple-element.9.f, f32[16,128]{1,0:T(8,128)S(1)} %get-tuple-element.10.g, f32[64,1024]{1,0:T(8,128)S(1)} %get-tuple-element.11.m), custom_call_target="tpu_custom_call" | custom-call | tf_op jit(solution)/shard_map/write_results/pallas_call | solution.py:581

commit v8 on v7

--- a/solution.py
+++ b/solution.py
@@ -17,7 +17,7 @@
 NZ, NX, NY = 8, 4, 8
 NC = 2 * NZ
 VMEM_GRANT = 56_150_000
-ROW_PARTS, COL_PARTS = 4, 2
+ROW_PARTS, COL_PARTS = 2, 2
 GROUP = 2
 
 
@@ -86,7 +86,7 @@
     c_mine,
     c_give,
     c_pair,
-    c_sum,
+    c_out,
     c_in,
     c_res,
     c_all,
@@ -422,41 +422,32 @@
     receive_b(1, COL_PARTS - 1)
 
 
-    def pair_copy(g):
-        part = pl.ds(g * GROUP, GROUP)
-        return copy(c_give.at[part], c_pair.at[part], s_p.at[0], r_p.at[g], partner)
-
     def finish_group(g):
         for i, res in enumerate(product(g * GROUP, GROUP, COL_PARTS - 1)):
             t = g * GROUP + i
             res = (res if COL_PARTS == 1 else m_acc[t] + res).T
-            c_mine[t, 0:half, :] = jnp.where(core == 0, res[:half], res[half:d])
-            c_give[t, 0:half, :] = jnp.where(core == 0, res[half:d], res[:half])
-            c_mine[t, half : half + 1, :] = res[d : d + 1]
-            c_give[t, half : half + 1, :] = res[d : d + 1]
-        pair_copy(g).start()
-
-    def merge_group(g):
-        pair_copy(g).wait_recv()
-        for t in range(g * GROUP, (g + 1) * GROUP):
             if order[t] == 0:
-                c_in[z] = c_mine[t] + c_pair[t]
+                c_in[z] = res[: d + 1]
             else:
-                c_sum[t] = c_mine[t] + c_pair[t]
+                c_out[t] = res[: d + 1]
         for t in range(g * GROUP, (g + 1) * GROUP):
             if order[t] != 0:
-                copy(c_sum.at[t], c_in.at[z], s_c.at[0], r_c.at[0], col_peer(order[t], 0)).start()
+                copy(c_out.at[t], c_in.at[z], s_c.at[0], r_c.at[0], col_peer(order[t], 0)).start()
 
     for g in range(NZ // GROUP):
         finish_group(g)
-        if g > 0:
-            merge_group(g - 1)
-    merge_group(NZ // GROUP - 1)
     got = c_in.at[0 : NZ - 1]
     c_whole = copy(got, got, s_c.at[0], r_c.at[0], peers[0])
     c_whole.wait_recv()
     tot = tree(jnp.add, [c_in[i] for i in range(NZ)])
-    c_res[...] = tot[:half] / tot[half : half + 1]
+    c_mine[0:half, :] = jnp.where(core == 0, tot[:half], tot[half:d])
+    c_give[0:half, :] = jnp.where(core == 0, tot[half:d], tot[:half])
+    c_mine[half : half + 1, :] = tot[d : d + 1]
+    c_give[half : half + 1, :] = tot[d : d + 1]
+    pair = copy(c_give, c_pair, s_p.at[0], r_p.at[0], partner)
+    pair.start()
+    pair.wait_recv()
+    c_res[...] = (c_mine[0:half] + c_pair[0:half]) / (c_mine[half:] + c_pair[half:])
 
     def gather_copy(o, k):
         return copy(c_res, c_all.at[core, z], s_g.at[0], r_g.at[o, k], col_peer(o, k))
@@ -482,7 +473,7 @@
         copy(a_got, a_got, s_a.at[step], r_a.at[step, 0], peers[0]).wait_send()
         copy(y_got, y_got, s_by.at[step], r_by.at[step, 0], peers[0]).wait_send()
         copy(x_got, x_got, s_bx.at[step], r_bx.at[step, 0], peers[0]).wait_send()
-    copy(c_give, c_give, s_p.at[0], r_p.at[0], partner).wait_send()
+    pair.wait_send()
     c_whole.wait_send()
     gather_copy(direct, 0).wait_recv()
     for o in range(NZ):
@@ -552,11 +543,11 @@
                 vmem((ITERS, COL_PARTS, NY, ntb // COL_PARTS, LANES), f32),
                 vmem((ITERS, COL_PARTS, ntb // COL_PARTS, LANES), f32),
                 vmem((ITERS, COL_PARTS, NX, ntb // COL_PARTS, LANES), f32),
-                vmem((NZ, half + 1, LANES), f32),
-                vmem((NZ, half + 1, LANES), f32),
-                vmem((NZ, half + 1, LANES), f32),
-                vmem((NZ, half + 1, LANES), f32),
-                vmem((NZ, half + 1, LANES), f32),
+                vmem((half + 1, LANES), f32),
+                vmem((half + 1, LANES), f32),
+                vmem((half + 1, LANES), f32),
+                vmem((NZ, d + 1, LANES), f32),
+                vmem((NZ, d + 1, LANES), f32),
                 vmem((half, LANES), f32),
                 vmem((2, NZ, half, LANES), f32),
                 dma((2,)),

time: 64.7 us -> 64.4 us (level)
  no operation moved by 1% of the time
where the time goes in v8:
time: 64.4 us; the launch traced here: 64.3 us
  Pallas kernels  63.5 us (99%)
  between operations  0.8 us (1%)
    pallas_call x1, Pallas kernels, shards(): pl.pallas_call(functools.partial(kernel, ns * nrow, nt * ncol), out_shape...  62.7 us

profile of v8, /device:TPU:1, one launch (start us, length us, event | category | flops | bytes accessed | tf_op | source)
XLA Modules:
  0.0 64.3 jit_solution(302699455904958258)
XLA Ops:
  0.6 62.7 %sinkhorn.1 = (f32[8,128]{1,0:T(8,128)S(1)}, f32[16,128]{1,0:T(8,128)S(1)}, f32[64,1024]{1,0:T(8,128)S(1)}) custom-call(f32[64,1024]{1,0:T(8,128)} %src_hbm.1, f32[64,2048]{1,0:T(8,128)} %tgt_hbm.1), custom_call_target="tpu_custom_call" | custom-call | tf_op jit(solution)/shard_map/sinkhorn/pallas_call | solution.py:511
  63.4 0.7 %write_results.1 = (f32[8,128]{1,0:T(8,128)}, f32[16,128]{1,0:T(8,128)}, f32[64,1024]{1,0:T(8,128)}) custom-call(f32[8,128]{1,0:T(8,128)S(1)} %get-tuple-element.9.f, f32[16,128]{1,0:T(8,128)S(1)} %get-tuple-element.10.g, f32[64,1024]{1,0:T(8,128)S(1)} %get-tuple-element.11.m), custom_call_target="tpu_custom_call" | custom-call | tf_op jit(solution)/shard_map/write_results/pallas_call | solution.py:572

commit v9 on v7

--- a/solution.py
+++ b/solution.py
@@ -17,7 +17,7 @@
 NZ, NX, NY = 8, 4, 8
 NC = 2 * NZ
 VMEM_GRANT = 56_150_000
-ROW_PARTS, COL_PARTS = 4, 2
+ROW_PARTS, COL_PARTS = 2, 2
 GROUP = 2
 
 
@@ -199,13 +199,20 @@
         part_m[rows, :] = top
         part_p[rows, :] = tree(jnp.add, [jnp.exp2(t - top) for t in ts])
 
+    def add_source_potential():
+        for b in range(ns // 32):
+            rows = slice(b * 32, (b + 1) * 32)
+            pot = fcol[rows, :]
+            for k in range(ntb):
+                lanes = slice(k * LANES, (k + 1) * LANES)
+                score[rows, lanes] += pot
+
     def plan_group(base, size, lo, hi):
         rows = pl.ds(base, size)
-        pot = fcol[rows, :]
         ps = []
         for k in range(lo, hi):
             lanes = slice(k * LANES, (k + 1) * LANES)
-            p = jnp.exp2((score[rows, lanes] + pot) + gpot[k : k + 1, :])
+            p = jnp.exp2(score[rows, lanes] + gpot[k : k + 1, :])
             plan[rows, lanes] = p
             ps.append(p)
         tot = tree(jnp.add, ps)
@@ -393,6 +400,7 @@
     first_row_pass()
     build_map_operand()
     col_pass(0)
+    add_source_potential()
     for c in range(COL_PARTS):
         relay_cols(0, c)
     later_row_pass(1)
@@ -465,14 +473,14 @@
         piece = c_all.at[core, (z + NZ - o) % NZ]
         return copy(piece, piece, s_g.at[0], r_g.at[o, 1], partner)
 
-    direct = NZ // 2
+    direct = [o for o in order if hops(o, NZ) > 2]
     for o in order[:-1]:
         gather_copy(o, 0).start()
-        if o == direct:
+        if o in direct:
             gather_copy(o, 1).start()
     gather_copy(0, 1).start()
     c_all[core, z] = c_res[...]
-    for o in order[::-1][1:-1]:
+    for o in [o for o in order[::-1] if o != 0 and o not in direct]:
         gather_copy(o, 0).wait_recv()
         relay_copy(o).start()
 
@@ -484,7 +492,8 @@
         copy(x_got, x_got, s_bx.at[step], r_bx.at[step, 0], peers[0]).wait_send()
     copy(c_give, c_give, s_p.at[0], r_p.at[0], partner).wait_send()
     c_whole.wait_send()
-    gather_copy(direct, 0).wait_recv()
+    for o in direct:
+        gather_copy(o, 0).wait_recv()
     for o in range(NZ):
         gather_copy(o, 1).wait_recv()
     for k in range(2):

time: 64.7 us -> 64.8 us (level)
  no operation moved by 1% of the time
where the time goes in v9:
time: 64.8 us; the launch traced here: 64.7 us
  Pallas kernels  63.9 us (99%)
  between operations  0.8 us (1%)
    pallas_call x1, Pallas kernels, shards(): pl.pallas_call(functools.partial(kernel, ns * nrow, nt * ncol), out_shape...  63.2 us

profile of v9, /device:TPU:1, one launch (start us, length us, event | category | flops | bytes accessed | tf_op | source)
XLA Modules:
  0.0 64.7 jit_solution(15740990456457769439)
XLA Ops:
  0.6 63.2 %sinkhorn.1 = (f32[8,128]{1,0:T(8,128)S(1)}, f32[16,128]{1,0:T(8,128)S(1)}, f32[64,1024]{1,0:T(8,128)S(1)}) custom-call(f32[64,1024]{1,0:T(8,128)} %src_hbm.1, f32[64,2048]{1,0:T(8,128)} %tgt_hbm.1), custom_call_target="tpu_custom_call" | custom-call | tf_op jit(solution)/shard_map/sinkhorn/pallas_call | solution.py:529
  63.8 0.7 %write_results.1 = (f32[8,128]{1,0:T(8,128)}, f32[16,128]{1,0:T(8,128)}, f32[64,1024]{1,0:T(8,128)}) custom-call(f32[8,128]{1,0:T(8,128)S(1)} %get-tuple-element.9.f, f32[16,128]{1,0:T(8,128)S(1)} %get-tuple-element.10.g, f32[64,1024]{1,0:T(8,128)S(1)} %get-tuple-element.11.m), custom_call_target="tpu_custom_call" | custom-call | tf_op jit(solution)/shard_map/write_results/pallas_call | solution.py:590
